TPU v7x, 512 devices: a whole 4x4x16 slice. The times are simulated.
512 devices in a mesh: chan: 8 (over x, y_hi), tm: 64 (over z, y_lo, core).
Axes of the slice: x: 4, y: 4 (y_hi: 2, y_lo: 2; y = y_hi * 2 + y_lo), z: 16, core: 2. Of those that a mesh axis runs over, the one named last changes fastest.
Arguments:
- launched: float32 [2, 96, 2, 524288], P(None, 'chan', None, 'tm'), may hold values from -6 to 6
- amp_noise: bfloat16 [2, 96, 2, 524288], P(None, 'chan', None, 'tm'), may hold values from -4 to 4
- window_start: int32 [96, 96], replicated, may hold values from -512 to 384, as said below
- window_length: int32 [96, 96], replicated, may hold values from 128 to 1024, as said below
Outputs:
- received: float32 [2, 96, 2, 524288], P(None, 'chan', None, 'tm')
Inputs may be any that keep to these rules, and one draw needn't show every extreme that they name: window_start: a multiple of 128; window_start + window_length <= 512 for every pair; for every channel c the pair (c, (c + 1) mod 96) has start -512. window_length: a multiple of 128; for every channel c the pair (c, (c + 1) mod 96) has length 1024.
All inputs are finite; a program needn't handle non-finite values.
Results may differ from a plain program's by a relative error of at most 0.0003.
Values sent between devices are 32-bit elements; how exact they have to be, the bound alone decides.
No kernel may reach another device: no remote copies, remote signals or barrier semaphores. Data moves between devices by JAX's collectives and lax.ppermute only.
A program may use at most 64 MiB of HBM per device.

v0:
```python
import jax
import jax.numpy as jnp
from jax import lax
from jax.sharding import PartitionSpec as P

HALO = 512


gamma_self = 0.1
gamma_cross = 0.05
highest = lax.Precision.HIGHEST


def extended_2(x, sides, width):
    for axis, dim in sides:
        peers, length = (lax.axis_size(axis), x.shape[dim])
        up = [(i, (i + 1) % peers) for i in range(peers)]
        down = [(j, i) for i, j in up]
        last = lax.slice_in_dim(x, length - width, length, axis=dim)
        leading = lax.slice_in_dim(x, 0, width, axis=dim)
        before = lax.ppermute(last, axis, up)
        after = lax.ppermute(leading, axis, down)
        x = jnp.concatenate([before, x, after], axis=dim)
    return x


def square_residue(signed_ids, modulus):
    base_value = signed_ids % modulus
    running = jnp.zeros_like(base_value)
    for shift_bits in (16, 8, 0):
        digit = base_value // (1 << shift_bits) % 256
        running = running * 256 % modulus
        running = (running + base_value * digit) % modulus
    return running


def rotation(left_ids, right_ids, period):
    product = left_ids[:, None] * right_ids[None, :] % period
    angles = product.astype(jnp.float32) * (2.0 * jnp.pi / period)
    return (jnp.cos(angles), jnp.sin(angles))


def apply_table(table, complex_pair, formula, conjugate):
    cosine, sine_part = table
    real_in, imag_in = complex_pair

    def product(matrix, values):
        return jnp.einsum(
            formula, matrix, values, precision=highest, preferred_element_type=jnp.float32
        )

    return (
        product(cosine, real_in) - conjugate * product(sine_part, imag_in),
        product(cosine, imag_in) + conjugate * product(sine_part, real_in),
    )


def apply_turn(table, complex_pair, conjugate):
    cosine, sine_part = table
    real_in, imag_in = complex_pair
    return (
        cosine * real_in - conjugate * sine_part * imag_in,
        cosine * imag_in + conjugate * sine_part * real_in,
    )


def regroup(complex_pair):
    return (
        lax.all_to_all(complex_pair[0], "tm", split_axis=1, concat_axis=1, tiled=True),
        lax.all_to_all(complex_pair[1], "tm", split_axis=1, concat_axis=1, tiled=True),
    )


def reshaped(complex_pair, shape):
    return (complex_pair[0].reshape(shape), complex_pair[1].reshape(shape))


def window_weights(starts, lengths, target_ids, source_ids):
    shift_count = 2 * HALO // 128
    offsets = (lax.iota(jnp.int32, shift_count) * 128 - HALO)[:, None, None]
    inside = (starts[None] <= offsets) & (offsets + 128 <= starts[None] + lengths[None])
    others = (target_ids[:, None] != source_ids[None, :])[None]
    inverse = 1.0 / lengths[None].astype(jnp.float32)
    return jnp.where(inside & others, inverse, jnp.zeros_like(inverse))


def slide_tables():
    rows_idx = lax.broadcasted_iota(jnp.int32, (128, 128), 0)
    cols_idx = lax.broadcasted_iota(jnp.int32, (128, 128), 1)
    return ((rows_idx >= cols_idx).astype(jnp.float32), (rows_idx < cols_idx).astype(jnp.float32))


def per_device(launched, amp_noise, window_start, window_length):
    groups = lax.axis_size("tm")
    tm_index = lax.axis_index("tm")
    chan_index = lax.axis_index("chan")
    local_chan = launched.shape[1]
    samples = launched.shape[3]
    channels = window_start.shape[0]
    row_count = local_chan * 2
    block_width = samples // groups
    length_all = samples * groups
    inner_blocks = samples // 128
    shift_count = 2 * HALO // 128
    working = reshaped((launched[0], launched[1]), (row_count, groups, block_width))
    working = regroup(working)
    group_ids = lax.iota(jnp.int32, groups)
    group_table = rotation(group_ids, group_ids, groups)
    working = apply_table(group_table, working, "kd,rdw->rkw", -1.0)
    sample_ids = tm_index * block_width + lax.iota(jnp.int32, block_width)
    outer_twiddle = rotation(group_ids, sample_ids, length_all)
    working = apply_turn(outer_twiddle, working, -1.0)
    working = regroup(working)
    working = reshaped(working, (row_count, inner_blocks, 128))
    block_ids = lax.iota(jnp.int32, inner_blocks)
    lane_ids = lax.iota(jnp.int32, 128)
    block_table = rotation(block_ids, block_ids, inner_blocks)
    lane_table = rotation(lane_ids, lane_ids, 128)
    inner_twiddle = rotation(block_ids, lane_ids, samples)
    working = apply_table(block_table, working, "ka,rab->rkb", -1.0)
    working = apply_turn(inner_twiddle, working, -1.0)
    working = apply_table(lane_table, working, "cb,rkb->rkc", -1.0)
    freq_ids = tm_index + groups * (block_ids[:, None] + inner_blocks * lane_ids[None, :])
    signed_ids = jnp.where(freq_ids < length_all // 2, freq_ids, freq_ids - length_all)
    modulus = 4 * length_all
    residue = square_residue(signed_ids, modulus)
    angles = residue.astype(jnp.float32) * (2.0 * jnp.pi / modulus)
    working = apply_turn((jnp.cos(angles), jnp.sin(angles)), working, 1.0)
    working = apply_table(lane_table, working, "cb,rkc->rkb", 1.0)
    working = apply_turn(inner_twiddle, working, 1.0)
    working = apply_table(block_table, working, "ka,rkb->rab", 1.0)
    working = reshaped(working, (row_count, groups, block_width))
    working = regroup(working)
    working = apply_turn(outer_twiddle, working, 1.0)
    working = apply_table(group_table, working, "kd,rkw->rdw", 1.0)
    working = regroup(working)
    real_part = working[0].reshape(local_chan, 2, samples) * (1.0 / length_all)
    imag_part = working[1].reshape(local_chan, 2, samples) * (1.0 / length_all)
    powers = jnp.sum(real_part * real_part + imag_part * imag_part, axis=1)
    extended = extended_2(powers, (("tm", 1),), HALO)
    block_total = extended.shape[1] // 128
    pieces = extended.reshape(local_chan, block_total, 128)
    upper_tri, lower_tri = slide_tables()
    sliding = jnp.einsum(
        "cnq,qr->cnr",
        pieces[:, :-1],
        upper_tri,
        precision=highest,
        preferred_element_type=jnp.float32,
    )
    sliding = sliding + jnp.einsum(
        "cnq,qr->cnr",
        pieces[:, 1:],
        lower_tri,
        precision=highest,
        preferred_element_type=jnp.float32,
    )
    sliding = sliding.reshape(local_chan, (block_total - 1) * 128)
    all_ids = lax.iota(jnp.int32, channels)
    local_ids = chan_index * local_chan + lax.iota(jnp.int32, local_chan)
    starts = lax.dynamic_slice_in_dim(window_start, chan_index * local_chan, local_chan, 0)
    lengths = lax.dynamic_slice_in_dim(window_length, chan_index * local_chan, local_chan, 0)
    weights_rows = window_weights(starts, lengths, local_ids, all_ids)
    running = jnp.zeros((local_chan, samples), jnp.float32)
    piece = lax.all_gather(sliding, "chan", axis=0, tiled=True)
    for offset_idx in range(shift_count):
        window_part = piece[:, 128 * offset_idx : 128 * offset_idx + samples]
        running = running + jnp.dot(
            weights_rows[offset_idx],
            window_part,
            precision=highest,
            preferred_element_type=jnp.float32,
        )
    phases = (gamma_self * powers + gamma_cross * running)[:, None, :]
    cosine = jnp.cos(phases)
    sine_part = jnp.sin(phases)
    out_real = cosine * real_part - sine_part * imag_part + amp_noise[0].astype(jnp.float32)
    out_imag = cosine * imag_part + sine_part * real_part + amp_noise[1].astype(jnp.float32)
    return jnp.stack([out_real, out_imag])


def solution(mesh):
    in_specs = (P(None, "chan", None, "tm"), P(None, "chan", None, "tm"), P(), P())
    out_specs = P(None, "chan", None, "tm")
    return jax.shard_map(
        per_device, mesh=mesh, in_specs=in_specs, out_specs=out_specs, check_vma=False
    )
```

profile of v0, /device:TPU:1, one launch (start us, length us, event | category | flops | bytes accessed | tf_op | source)
XLA Modules:
  0.0 567.8 jit_solution(962996634951794186)
XLA Ops:
  10.0 18.2 %all-to-all-start = ((f32[24,64,128]{2,0,1:T(8,128)}), f32[24,64,128]{2,0,1:T(8,128)S(1)}, u32[]{:S(2)}, u32[]{:S(2)}) async-start(f32[24,64,128]{2,0,1:T(8,128)} %copy.47), calls=%async_computation | async-start | bytes 1572864 | tf_op jit(solution)/shard_map/all_to_all | solution.py:69
  30.3 41.1 %all-to-all-done = f32[24,64,128]{2,0,1:T(8,128)S(1)} async-done(((f32[24,64,128]{2,0,1:T(8,128)}), f32[24,64,128]{2,0,1:T(8,128)S(1)}, u32[]{:S(2)}, u32[]{:S(2)}) %all-to-all-start) | async-done | bytes 786464 | tf_op jit(solution)/shard_map/all_to_all | solution.py:69
  71.3 6.3 %all-to-all-start.1 = ((f32[24,64,128]{2,0,1:T(8,128)}), f32[24,64,128]{2,0,1:T(8,128)S(1)}, u32[]{:S(2)}, u32[]{:S(2)}) async-start(f32[24,64,128]{2,0,1:T(8,128)} %copy.50), calls=%async_computation.1 | async-start | bytes 1572864 | tf_op jit(solution)/shard_map/all_to_all | solution.py:70
  78.8 42.0 %all-to-all-done.1 = f32[24,64,128]{2,0,1:T(8,128)S(1)} async-done(((f32[24,64,128]{2,0,1:T(8,128)}), f32[24,64,128]{2,0,1:T(8,128)S(1)}, u32[]{:S(2)}, u32[]{:S(2)}) %all-to-all-start.1) | async-done | bytes 786464 | tf_op jit(solution)/shard_map/all_to_all | solution.py:70
  125.3 6.4 %all-to-all-start.2 = ((f32[24,64,128]{2,0,1:T(8,128)}), f32[24,64,128]{2,0,1:T(8,128)S(1)}, u32[]{:S(2)}, u32[]{:S(2)}) async-start(f32[24,64,128]{2,0,1:T(8,128)} %copy.57), calls=%async_computation.2 | async-start | bytes 1572864 | tf_op jit(solution)/shard_map/all_to_all | solution.py:69
  133.0 41.8 %all-to-all-done.2 = f32[24,64,128]{2,0,1:T(8,128)S(1)} async-done(((f32[24,64,128]{2,0,1:T(8,128)}), f32[24,64,128]{2,0,1:T(8,128)S(1)}, u32[]{:S(2)}, u32[]{:S(2)}) %all-to-all-start.2) | async-done | bytes 786464 | tf_op jit(solution)/shard_map/all_to_all | solution.py:69
  174.9 6.6 %all-to-all-start.3 = ((f32[24,64,128]{2,0,1:T(8,128)}), f32[24,64,128]{2,0,1:T(8,128)S(1)}, u32[]{:S(2)}, u32[]{:S(2)}) async-start(f32[24,64,128]{2,0,1:T(8,128)} %copy.60), calls=%async_computation.3 | async-start | bytes 1572864 | tf_op jit(solution)/shard_map/all_to_all | solution.py:70
  183.1 41.4 %all-to-all-done.3 = f32[24,64,128]{2,0,1:T(8,128)S(1)} async-done(((f32[24,64,128]{2,0,1:T(8,128)}), f32[24,64,128]{2,0,1:T(8,128)S(1)}, u32[]{:S(2)}, u32[]{:S(2)}) %all-to-all-start.3) | async-done | bytes 786464 | tf_op jit(solution)/shard_map/all_to_all | solution.py:70
  239.4 6.4 %all-to-all-start.5 = ((f32[24,64,128]{2,0,1:T(8,128)}), f32[24,64,128]{2,0,1:T(8,128)S(1)}, u32[]{:S(2)}, u32[]{:S(2)}) async-start(f32[24,64,128]{2,0,1:T(8,128)} %copy.68), calls=%async_computation.5 | async-start | bytes 1572864 | tf_op jit(solution)/shard_map/all_to_all | solution.py:70
  248.4 40.6 %all-to-all-done.5 = f32[24,64,128]{2,0,1:T(8,128)S(1)} async-done(((f32[24,64,128]{2,0,1:T(8,128)}), f32[24,64,128]{2,0,1:T(8,128)S(1)}, u32[]{:S(2)}, u32[]{:S(2)}) %all-to-all-start.5) | async-done | bytes 786464 | tf_op jit(solution)/shard_map/all_to_all | solution.py:70
  289.0 48.7 %all_to_all.40 = f32[24,64,128]{2,0,1:T(8,128)S(1)} all-to-all(f32[24,64,128]{2,0,1:T(8,128)S(1)} %copy.67), channel_id=1, replica_groups=mesh['chan'=8,'tm'=64] {'tm'}, dimensions={1} | all-to-all | bytes 1572864 | tf_op jit(solution)/shard_map/all_to_all | solution.py:69
  341.3 6.4 %all-to-all-start.6 = ((f32[24,64,128]{2,0,1:T(8,128)}), f32[24,64,128]{2,0,1:T(8,128)S(1)}, u32[]{:S(2)}, u32[]{:S(2)}) async-start(f32[24,64,128]{2,0,1:T(8,128)} %copy.71), calls=%async_computation.6 | async-start | bytes 1572864 | tf_op jit(solution)/shard_map/all_to_all | solution.py:69
  350.6 40.2 %all-to-all-done.6 = f32[24,64,128]{2,0,1:T(8,128)S(1)} async-done(((f32[24,64,128]{2,0,1:T(8,128)}), f32[24,64,128]{2,0,1:T(8,128)S(1)}, u32[]{:S(2)}, u32[]{:S(2)}) %all-to-all-start.6) | async-done | bytes 786464 | tf_op jit(solution)/shard_map/all_to_all | solution.py:69
  390.9 48.7 %all_to_all.41 = f32[24,64,128]{2,0,1:T(8,128)S(1)} all-to-all(f32[24,64,128]{2,0,1:T(8,128)S(1)} %copy.75), channel_id=1, replica_groups=mesh['chan'=8,'tm'=64] {'tm'}, dimensions={1} | all-to-all | bytes 1572864 | tf_op jit(solution)/shard_map/all_to_all | solution.py:70
  443.3 5.3 collective-permute-start
  448.6 1.9 collective-permute-start.1
  450.6 3.3 collective-permute-done.1
  460.4 79.5 %all-gather.3.cloned.1.call-done = f32[8,12,9088]{2,1,0:T(8,128)} async-done(((f32[1,12,9088]{2,1,0:T(8,128)}), f32[8,12,9088]{2,1,0:T(8,128)}) %all-gather.3.cloned.1.call-update) | async-done | bytes 3489808 | tf_op jit(solution)/shard_map/all_gather | solution.py:165
  539.9 2.7 reshape.417
  544.3 1.6 convolution_add_fusion.6
  545.9 1.6 convolution_add_fusion.5
  547.5 1.6 convolution_add_fusion.4
  554.0 3.6 cosine_multiply_fusion
  558.8 2.0 pad_maximum_fusion
  (81 shorter events, 55.6 us)
Async XLA Ops:
  10.0 61.3 %all-to-all-start = ((f32[24,64,128]{2,0,1:T(8,128)}), f32[24,64,128]{2,0,1:T(8,128)S(1)}, u32[]{:S(2)}, u32[]{:S(2)}) async-start(f32[24,64,128]{2,0,1:T(8,128)} %copy.47), calls=%async_computation | async-start | bytes 1572864 | tf_op jit(solution)/shard_map/all_to_all | solution.py:69
  71.3 49.5 %all-to-all-start.1 = ((f32[24,64,128]{2,0,1:T(8,128)}), f32[24,64,128]{2,0,1:T(8,128)S(1)}, u32[]{:S(2)}, u32[]{:S(2)}) async-start(f32[24,64,128]{2,0,1:T(8,128)} %copy.50), calls=%async_computation.1 | async-start | bytes 1572864 | tf_op jit(solution)/shard_map/all_to_all | solution.py:70
  125.3 49.6 %all-to-all-start.2 = ((f32[24,64,128]{2,0,1:T(8,128)}), f32[24,64,128]{2,0,1:T(8,128)S(1)}, u32[]{:S(2)}, u32[]{:S(2)}) async-start(f32[24,64,128]{2,0,1:T(8,128)} %copy.57), calls=%async_computation.2 | async-start | bytes 1572864 | tf_op jit(solution)/shard_map/all_to_all | solution.py:69
  174.9 49.6 %all-to-all-start.3 = ((f32[24,64,128]{2,0,1:T(8,128)}), f32[24,64,128]{2,0,1:T(8,128)S(1)}, u32[]{:S(2)}, u32[]{:S(2)}) async-start(f32[24,64,128]{2,0,1:T(8,128)} %copy.60), calls=%async_computation.3 | async-start | bytes 1572864 | tf_op jit(solution)/shard_map/all_to_all | solution.py:70
  239.4 49.6 %all-to-all-start.5 = ((f32[24,64,128]{2,0,1:T(8,128)}), f32[24,64,128]{2,0,1:T(8,128)S(1)}, u32[]{:S(2)}, u32[]{:S(2)}) async-start(f32[24,64,128]{2,0,1:T(8,128)} %copy.68), calls=%async_computation.5 | async-start | bytes 1572864 | tf_op jit(solution)/shard_map/all_to_all | solution.py:70
  341.3 49.6 %all-to-all-start.6 = ((f32[24,64,128]{2,0,1:T(8,128)}), f32[24,64,128]{2,0,1:T(8,128)S(1)}, u32[]{:S(2)}, u32[]{:S(2)}) async-start(f32[24,64,128]{2,0,1:T(8,128)} %copy.71), calls=%async_computation.6 | async-start | bytes 1572864 | tf_op jit(solution)/shard_map/all_to_all | solution.py:69
  347.7 192.3 %all-gather.3.cloned.1.call-start = ((), (), s32[]{:S(2)}) async-start(), calls=%async_computation.8 | async-start | bytes 5234688 | tf_op jit(solution)/shard_map/all_gather | solution.py:165
  443.3 12.4 %copy-start = (f32[12,8192]{1,0:T(8,128)}, f32[12,8192]{1,0:T(8,128)S(1)}, u32[]{:S(2)}) copy-start(f32[12,8192]{1,0:T(8,128)S(1)} %reduce_sum.9) | copy-start | bytes 1179652
  443.3 7.3 %collective-permute-start = (f32[12,512]{1,0:T(8,128)S(1)}, f32[12,512]{1,0:T(8,128)S(1)}, u32[]{:S(2)}, u32[]{:S(2)}) collective-permute-start(f32[12,512]{1,0:T(8,128)S(1)} %get-tuple-element.15), channel_id=1, source_target_pairs={{0,1},{1,2},{2,3},{3,4},{4,5},{5,6},{6,7},{7,8},{8,9},{9,10},{10,1... | collective-permute-start | bytes 73736 | tf_op jit(solution)/shard_map/ppermute | solution.py:21
  448.6 5.2 collective-permute-start.1
  552.3 1.6 copy-start.1
  553.9 3.6 copy-start.2
  554.0 3.6 copy-start.3
  554.0 3.6 copy-start.4
Sparse Core Ops, SparseCore 0:
  455.8 84.0 all-gather.2
where the time goes:
time: 577 us; the launch traced here: 568 us
  waiting for transfers between devices  330 us (57%)
  blocking collectives  97.5 us (17%)
  starting transfers between devices  58 us (10%)
  matrix products  40.1 us (7%)
  local copies, waits for them, and re-layouts  21.3 us (4%)
  between operations  14.2 us (2%)
  other arithmetic  6.82 us (1%)
    all_to_all x3, waiting for transfers between devices, regroup(): lax.all_to_all(complex_pair[1], 'tm', split_axis=1, concat_axis=1, tiled=...  124 us
    all_to_all x3, waiting for transfers between devices, regroup(): lax.all_to_all(complex_pair[0], 'tm', split_axis=1, concat_axis=1, tiled=...  123 us
    all_gather x1, waiting for transfers between devices, per_device(): piece = lax.all_gather(sliding, 'chan', axis=0, tiled=True)  79.5 us
    all_to_all x1, blocking collectives, regroup(): lax.all_to_all(complex_pair[1], 'tm', split_axis=1, concat_axis=1, tiled=...  48.7 us
    all_to_all x1, blocking collectives, regroup(): lax.all_to_all(complex_pair[0], 'tm', split_axis=1, concat_axis=1, tiled=...  48.7 us
    all_to_all x3, starting transfers between devices, regroup(): lax.all_to_all(complex_pair[0], 'tm', split_axis=1, concat_axis=1, tiled=...  31 us
    dot_general x24, matrix products, product(): jnp.einsum(formula, matrix, values, precision=highest, preferred_element_...  24.6 us
    all_to_all x3, starting transfers between devices, regroup(): lax.all_to_all(complex_pair[1], 'tm', split_axis=1, concat_axis=1, tiled=...  19.3 us
  transfers between devices with their start and end apart: 9, of which 8 were waited for; matrix products, arithmetic and copies ran while one was open for 3% of the time, Pallas kernels for 0%

commit v1 on v0

v1 whole, which is shorter than its diff:
```python
import functools

import jax
import jax.numpy as jnp
import ml_dtypes
import numpy as np
from jax import lax
from jax.experimental import pallas as pl
from jax.experimental.pallas import tpu as pltpu
from jax.sharding import Mesh
from jax.sharding import PartitionSpec as P

HALO = 512
GAMMA_SELF = 0.1
GAMMA_CROSS = 0.05
SAMPLES = 524288
LANES = 128
COARSE = 8
FOLDED = SAMPLES // COARSE
OUTER = FOLDED // LANES
highest = lax.Precision.HIGHEST


def split_np(matrix):
    upper = matrix.astype(ml_dtypes.bfloat16)
    lower = (matrix - upper.astype(np.float64)).astype(ml_dtypes.bfloat16)
    return np.stack([upper, lower])


def roots(numerators, period):
    angles = (numerators % period) * (2.0 * np.pi / period)
    return np.cos(angles), np.sin(angles)


@functools.cache
def tables():
    outer_ids = np.arange(OUTER, dtype=np.int64)
    lane_ids = np.arange(LANES, dtype=np.int64)
    residues = np.arange(COARSE, dtype=np.int64)
    cosine, sine = roots(outer_ids[:, None] * outer_ids[None, :], OUTER)
    outer = np.stack([split_np(cosine), split_np(sine)])
    cosine, sine = roots(lane_ids[:, None] * lane_ids[None, :], LANES)
    forward = np.block([[cosine, -sine], [sine, cosine]])
    inner = np.stack([split_np(forward), split_np(forward.T)])
    turn = np.stack(roots(outer_ids[:, None] * lane_ids[None, :], FOLDED)).astype(np.float32)
    time_ids = LANES * outer_ids[:, None] + lane_ids[None, :]
    shift = np.stack(roots(residues[:, None, None] * time_ids[None], SAMPLES), axis=1)
    freq_ids = residues[:, None, None] + COARSE * (
        outer_ids[None, :, None] + OUTER * lane_ids[None, None, :]
    )
    signed_ids = np.where(freq_ids < SAMPLES // 2, freq_ids, freq_ids - SAMPLES)
    response = np.stack(roots(signed_ids * signed_ids, 4 * SAMPLES), axis=1) / SAMPLES
    return outer, inner, turn, shift.astype(np.float32), response.astype(np.float32)


def radix_eight(parts, sign):
    half = np.float32(np.sqrt(0.5))

    def add(a, b):
        return a[0] + b[0], a[1] + b[1]

    def sub(a, b):
        return a[0] - b[0], a[1] - b[1]

    def quarter(a):
        return (-sign * a[1], sign * a[0])

    def eighth(a):
        return (half * (a[0] - sign * a[1]), half * (a[1] + sign * a[0]))

    def four(a, b, c, d):
        even_sum, even_diff = add(a, c), sub(a, c)
        odd_sum, odd_diff = add(b, d), quarter(sub(b, d))
        return (
            add(even_sum, odd_sum),
            add(even_diff, odd_diff),
            sub(even_sum, odd_sum),
            sub(even_diff, odd_diff),
        )

    even = four(*(add(parts[i], parts[i + 4]) for i in range(4)))
    diffs = [sub(parts[i], parts[i + 4]) for i in range(4)]
    odd = four(
        diffs[0], eighth(diffs[1]), quarter(diffs[2]), quarter(eighth(diffs[3]))
    )
    return [pair for both in zip(even, odd) for pair in both]


def fold_kernel(sign, in_ref, out_ref):
    rows = 8

    @pl.loop(0, in_ref.shape[3] // rows)
    def _(step):
        at = pl.ds(pl.multiple_of(step * rows, rows), rows)
        parts = [(in_ref[i, 0, 0, at, :], in_ref[i, 1, 0, at, :]) for i in range(COARSE)]
        for i, pair in enumerate(radix_eight(parts, sign)):
            out_ref[i, 0, 0, at, :] = pair[0]
            out_ref[i, 1, 0, at, :] = pair[1]


def fold(values, sign):
    spec = pl.BlockSpec((8, 2, 1, 64, 128), lambda row: (0, 0, row, 0, 0))
    return pl.pallas_call(
        functools.partial(fold_kernel, sign),
        grid=(values.shape[2],),
        in_specs=[spec],
        out_specs=spec,
        out_shape=jax.ShapeDtypeStruct(values.shape, jnp.float32),
    )(values)


def halves(values):
    upper = values.astype(jnp.bfloat16)
    lower = (values - upper.astype(jnp.float32)).astype(jnp.bfloat16)
    return upper, lower


def dot(left, right):
    return jnp.dot(left, right, preferred_element_type=jnp.float32)


def triple(left, right):
    return dot(left[0], right[0]) + (dot(left[0], right[1]) + dot(left[1], right[0]))


def disperse_kernel(
    residue_ref, in_ref, outer_ref, inner_ref, turn_ref, shift_ref, response_ref, out_ref
):
    def turned(real, imag, cosine, sine, sign):
        if sign > 0:
            return real * cosine - imag * sine, imag * cosine + real * sine
        return real * cosine + imag * sine, imag * cosine - real * sine

    def packed(real, imag):
        return halves(jnp.concatenate([real, imag], axis=1))

    cosines = (outer_ref[0, 0], outer_ref[0, 1])
    sines = (outer_ref[1, 0], outer_ref[1, 1])
    shift = (shift_ref[0, 0], shift_ref[0, 1])
    turn = (turn_ref[0], turn_ref[1])
    real = in_ref[:, 0, 0].reshape(OUTER, LANES)
    imag = in_ref[:, 1, 0].reshape(OUTER, LANES)
    values = packed(*turned(real, imag, *shift, -1))
    by_cos, by_sin = triple(cosines, values), triple(sines, values)
    real = by_cos[:, :LANES] + by_sin[:, LANES:]
    imag = by_cos[:, LANES:] - by_sin[:, :LANES]
    values = packed(*turned(real, imag, *turn, -1))
    both = triple(values, (inner_ref[0, 0], inner_ref[0, 1]))
    real, imag = turned(
        both[:, :LANES], both[:, LANES:], response_ref[0, 0], response_ref[0, 1], 1
    )
    both = triple(packed(real, imag), (inner_ref[1, 0], inner_ref[1, 1]))
    values = packed(*turned(both[:, :LANES], both[:, LANES:], *turn, 1))
    by_cos, by_sin = triple(cosines, values), triple(sines, values)
    real = by_cos[:, :LANES] - by_sin[:, LANES:]
    imag = by_cos[:, LANES:] + by_sin[:, :LANES]
    real, imag = turned(real, imag, *shift, 1)
    out_ref[:, 0, 0] = real.reshape(8, 64, LANES)
    out_ref[:, 1, 0] = imag.reshape(8, 64, LANES)


def disperse(values, residue):
    spec = pl.BlockSpec((8, 2, 1, 64, 128), lambda row, res: (0, 0, row, 0, 0))
    outer, inner, turn, shift, response = tables()

    def whole(table):
        return pl.BlockSpec(table.shape, lambda row, res: (0,) * table.ndim)

    def one_residue(table):
        return pl.BlockSpec((1,) + table.shape[1:], lambda row, res: (res[0], 0, 0, 0))

    return pl.pallas_call(
        disperse_kernel,
        grid_spec=pltpu.PrefetchScalarGridSpec(
            num_scalar_prefetch=1,
            grid=(values.shape[2],),
            in_specs=[
                spec,
                whole(outer),
                whole(inner),
                whole(turn),
                one_residue(shift),
                one_residue(response),
            ],
            out_specs=spec,
        ),
        out_shape=jax.ShapeDtypeStruct(values.shape, jnp.float32),
        compiler_params=pltpu.CompilerParams(vmem_limit_bytes=40 * 1024 * 1024),
    )(residue, values, outer, inner, turn, shift, response)


def window_weights(starts, lengths):
    channels = starts.shape[0]
    shift_count = 2 * HALO // 128
    offsets = (lax.iota(jnp.int32, shift_count) * 128 - HALO)[None, :, None]
    starts, lengths = starts[:, None, :], lengths[:, None, :]
    inside = (starts <= offsets) & (offsets + 128 <= starts + lengths)
    ids = lax.iota(jnp.int32, channels)
    others = (ids[:, None] != ids[None, :])[:, None, :]
    inverse = 1.0 / lengths.astype(jnp.float32)
    weights = jnp.where(inside & others, inverse, jnp.zeros_like(inverse))
    return weights.reshape(channels, shift_count * channels)


def cross_kernel(weights_ref, in_ref, out_ref):
    weights = halves(weights_ref[...])
    channels, depth = weights_ref.shape
    for step in range(out_ref.shape[1]):
        values = halves(in_ref[step * channels : step * channels + depth, :])
        out_ref[:, step, :] = triple(weights, values)


def slide_tables():
    rows_idx = lax.broadcasted_iota(jnp.int32, (128, 128), 0)
    cols_idx = lax.broadcasted_iota(jnp.int32, (128, 128), 1)
    return ((rows_idx >= cols_idx).astype(jnp.float32), (rows_idx < cols_idx).astype(jnp.float32))


def exchange(values, axis):
    return lax.all_to_all(values, axis, 0, 0, tiled=True)


def per_device(launched, amp_noise, window_start, window_length):
    channels = window_start.shape[0]
    local_chan = launched.shape[1]
    rows = 2 * local_chan
    blocks = launched.shape[3] // LANES
    residue = lax.axis_index("i").astype(jnp.int32).reshape(1)
    values = launched.reshape(2, COARSE, rows // COARSE, blocks, LANES).transpose(1, 0, 2, 3, 4)
    values = exchange(values, "j")
    values = fold(values, -1)
    values = exchange(values, "i")
    values = disperse(values, residue)
    values = exchange(values, "i")
    values = fold(values, 1)
    values = exchange(values, "j")
    fields = values.transpose(1, 0, 2, 3, 4).reshape(2, local_chan, 2, blocks, LANES)
    powers = jnp.sum(fields * fields, axis=(0, 2))
    count = lax.axis_size("j") * lax.axis_size("i")
    up = [(k, (k + 1) % count) for k in range(count)]
    down = [(k, j) for j, k in up]
    reach = HALO // LANES
    before = lax.ppermute(powers[:, blocks - reach :], ("j", "i"), up)
    after = lax.ppermute(powers[:, :reach], ("j", "i"), down)
    extended = jnp.concatenate([before, powers, after], axis=1)
    upper_tri, lower_tri = slide_tables()
    sliding = jnp.einsum("cnq,qr->cnr", extended[:, :-1], upper_tri, precision=highest)
    sliding = sliding + jnp.einsum("cnq,qr->cnr", extended[:, 1:], lower_tri, precision=highest)
    groups = lax.axis_size("chan")
    own = blocks // groups
    taken = own + 2 * reach - 1
    pieces = jnp.stack([sliding[:, own * k : own * k + taken] for k in range(groups)])
    pieces = exchange(pieces, "chan")
    pieces = pieces.transpose(2, 0, 1, 3).reshape(taken * channels, LANES)
    weights = window_weights(window_start, window_length)
    cross = pl.pallas_call(
        cross_kernel,
        out_shape=jax.ShapeDtypeStruct((channels, own, LANES), jnp.float32),
    )(weights, pieces)
    cross = exchange(cross.reshape(groups, local_chan, own, LANES), "chan")
    cross = cross.transpose(1, 0, 2, 3).reshape(local_chan, blocks, LANES)
    phases = (GAMMA_SELF * powers + GAMMA_CROSS * cross)[:, None]
    cosine, sine = jnp.cos(phases), jnp.sin(phases)
    out_real = cosine * fields[0] - sine * fields[1]
    out_imag = cosine * fields[1] + sine * fields[0]
    received = jnp.stack([out_real, out_imag]).reshape(launched.shape)
    return received + amp_noise.astype(jnp.float32)


def solution(mesh):
    split = Mesh(mesh.devices.reshape(mesh.shape["chan"], COARSE, -1), ("chan", "j", "i"))
    fields = P(None, "chan", None, ("j", "i"))
    return jax.shard_map(
        per_device,
        mesh=split,
        in_specs=(fields, fields, P(), P()),
        out_specs=fields,
        check_vma=False,
    )
```

time: 577 us -> 303 us (0.53)
  the two profiles are of different devices: /device:TPU:1 before, /device:TPU:64 now
where the time goes in v1:
time: 303 us; the launch traced here: 302 us
  blocking collectives  194 us (64%)
  waiting for transfers between devices  38 us (13%)
  starting transfers between devices  21.1 us (7%)
  local copies, waits for them, and re-layouts  20 us (7%)
  Pallas kernels  19.6 us (6%)
  other arithmetic  7.6 us (3%)
    all_to_all x3, blocking collectives, exchange(): return lax.all_to_all(values, axis, 0, 0, tiled=True)  194 us
    all_to_all x3, waiting for transfers between devices, exchange(): return lax.all_to_all(values, axis, 0, 0, tiled=True)  36.5 us
    all_to_all x3, starting transfers between devices, exchange(): return lax.all_to_all(values, axis, 0, 0, tiled=True)  14.6 us
    unnamed x29, local copies, waits for them, and re-layouts  10.8 us
    pallas_call x1, Pallas kernels, disperse(): pl.pallas_call(disperse_kernel, grid_spec=pltpu.PrefetchScalarGridSpec(nu...  9.32 us
    pallas_call x2, Pallas kernels, fold(): pl.pallas_call(functools.partial(fold_kernel, sign), grid=(values.shape[2...  7.13 us
  transfers between devices with their start and end apart: 5, of which 4 were waited for; matrix products, arithmetic and copies ran while one was open for 2% of the time, Pallas kernels for 0%

profile of v1, /device:TPU:64, one launch (start us, length us, event | category | flops | bytes accessed | tf_op | source)
XLA Modules:
  0.0 301.7 jit_solution(12170265423927872073)
XLA Ops:
  0.0 2.6 reshape.139
  2.7 90.7 %all_to_all.30.in_ref = f32[8,2,3,64,128]{4,3,2,1,0:T(8,128)} all-to-all(f32[8,2,3,64,128]{4,3,2,1,0:T(8,128)S(1)} %bitcast.67), channel_id=1, replica_groups=mesh['chan'=8,'j'=8,'i'=8] {'j'}, dimensions={0} | all-to-all | bytes 3145728 | tf_op jit(solution)/shard_map/all_to_all | solution.py:220
  93.5 3.6 %shard_map.91 = f32[8,2,3,64,128]{4,3,2,1,0:T(8,128)} custom-call(f32[8,2,3,64,128]{4,3,2,1,0:T(8,128)} %all_to_all.30.in_ref), custom_call_target="tpu_custom_call" | custom-call | tf_op jit(solution)/shard_map/pallas_call | solution.py:103
  97.1 3.7 %all-to-all-start.1 = ((f32[8,2,3,64,128]{4,3,2,1,0:T(8,128)}), f32[8,2,3,64,128]{4,3,2,1,0:T(8,128)S(1)}, u32[]{:S(2)}, u32[]{:S(2)}) async-start(f32[8,2,3,64,128]{4,3,2,1,0:T(8,128)} %shard_map.91), calls=%async_computation.1 | async-start | bytes 3145728 | tf_op jit(solution)/shard_map/all_to_all | solution.py:220
  100.8 20.0 %all-to-all-done.1.in_ref = f32[8,2,3,64,128]{4,3,2,1,0:T(8,128)S(1)} async-done(((f32[8,2,3,64,128]{4,3,2,1,0:T(8,128)}), f32[8,2,3,64,128]{4,3,2,1,0:T(8,128)S(1)}, u32[]{:S(2)}, u32[]{:S(2)}) %all-to-all-start.1) | async-done | bytes 1572896 | tf_op jit(solution)/shard_map/all_to_all | solution.py:220
  120.8 2.2 copy-done
  123.0 1.6 copy-done.1
  124.6 9.3 %shard_map.92 = f32[8,2,3,64,128]{4,3,2,1,0:T(8,128)S(1)} custom-call(s32[1]{0:T(128)} %bitcast.residue_ref, f32[8,2,3,64,128]{4,3,2,1,0:T(8,128)S(1)} %all-to-all-done.1.in_ref, bf16[2,2,512,512]{3,2,1,0:T(8,128)(2,1)S(1)} %copy-done.1, bf16[2,2,256,256]{3,2,1,0:T(8,128)(2,1)S(1)} %copy-done.2, f32[2,512,128]{2,1,0:T(8,128)S(1)} %copy-done.3, ...), custom_call_target="tpu_custom_call" | custom-call | tf_op jit(solution)/shard_map/pallas_call | solution.py:172
  133.9 23.4 %all_to_all.31.in_ref = f32[8,2,3,64,128]{4,3,2,1,0:T(8,128)} all-to-all(f32[8,2,3,64,128]{4,3,2,1,0:T(8,128)S(1)} %shard_map.92), channel_id=1, replica_groups=mesh['chan'=8,'j'=8,'i'=8] {'i'}, dimensions={0} | all-to-all | bytes 3145728 | tf_op jit(solution)/shard_map/all_to_all | solution.py:220
  157.3 3.6 %shard_map.93 = f32[8,2,3,64,128]{4,3,2,1,0:T(8,128)} custom-call(f32[8,2,3,64,128]{4,3,2,1,0:T(8,128)} %all_to_all.31.in_ref), custom_call_target="tpu_custom_call" | custom-call | tf_op jit(solution)/shard_map/pallas_call | solution.py:103
  160.9 80.3 %all_to_all.32 = f32[8,2,3,64,128]{4,3,2,1,0:T(8,128)S(1)} all-to-all(f32[8,2,3,64,128]{4,3,2,1,0:T(8,128)} %shard_map.93), channel_id=1, replica_groups=mesh['chan'=8,'j'=8,'i'=8] {'j'}, dimensions={0} | all-to-all | bytes 3145728 | tf_op jit(solution)/shard_map/all_to_all | solution.py:220
  241.5 1.9 collective-permute-start
  243.4 4.5 %collective-permute-start.1 = (f32[12,4,128]{2,1,0:T(4,128)S(1)}, f32[12,4,128]{2,1,0:T(4,128)S(1)}, u32[]{:S(2)}, u32[]{:S(2)}) collective-permute-start(f32[12,4,128]{2,1,0:T(4,128)S(1)} %get-tuple-element.12), channel_id=1, source_target_pairs={{1,0},{2,1},{3,2},{4,3},{5,4},{6,5},{7,6},{8,7},{9,8},{10,9},{11,1... | collective-permute-start | bytes 73736 | tf_op jit(solution)/shard_map/ppermute | solution.py:244
  247.9 1.5 collective-permute-done.1
  255.4 6.9 %all-to-all-start.4 = ((f32[8,12,15,128]{3,2,1,0:T(8,128)}), f32[8,12,15,128]{3,2,1,0:T(8,128)S(1)}, u32[]{:S(2)}, u32[]{:S(2)}) async-start(f32[8,12,15,128]{3,2,1,0:T(8,128)} %fusion.3), calls=%async_computation.4 | async-start | bytes 1572864 | tf_op jit(solution)/shard_map/all_to_all | solution.py:220
  265.0 1.8 and_select_fusion.weights_ref
  266.8 9.2 %all-to-all-done.4 = f32[8,12,15,128]{3,2,1,0:T(8,128)S(1)} async-done(((f32[8,12,15,128]{3,2,1,0:T(8,128)}), f32[8,12,15,128]{3,2,1,0:T(8,128)S(1)}, u32[]{:S(2)}, u32[]{:S(2)}) %all-to-all-start.4) | async-done | bytes 737312 | tf_op jit(solution)/shard_map/all_to_all | solution.py:220
  276.9 1.4 copy.18
  279.2 3.1 %shard_map.94 = f32[96,8,128]{2,1,0:T(8,128)} custom-call(f32[96,768]{1,0:T(8,128)} %and_select_fusion.weights_ref, f32[1440,128]{1,0:T(8,128)} %reshape.140.in_ref), custom_call_target="tpu_custom_call" | custom-call | tf_op jit(solution)/shard_map/pallas_call | solution.py:256
  282.3 4.0 %all-to-all-start.5 = ((f32[8,12,8,128]{3,2,1,0:T(8,128)}), f32[8,12,8,128]{3,2,1,0:T(8,128)S(1)}, u32[]{:S(2)}, u32[]{:S(2)}) async-start(f32[8,12,8,128]{3,2,1,0:T(8,128)} %bitcast.74), calls=%async_computation.5 | async-start | bytes 786432 | tf_op jit(solution)/shard_map/all_to_all | solution.py:220
  286.4 1.1 copy.20
  288.5 7.3 %all-to-all-done.5 = f32[8,12,8,128]{3,2,1,0:T(8,128)S(1)} async-done(((f32[8,12,8,128]{3,2,1,0:T(8,128)}), f32[8,12,8,128]{3,2,1,0:T(8,128)S(1)}, u32[]{:S(2)}, u32[]{:S(2)}) %all-to-all-start.5) | async-done | bytes 393248 | tf_op jit(solution)/shard_map/all_to_all | solution.py:220
  296.2 1.9 add_cosine_fusion
  299.3 2.4 maximum_add_fusion
  (59 shorter events, 13.2 us)
Async XLA Ops:
  97.1 23.7 %copy-start.2 = (bf16[2,2,256,256]{3,2,1,0:T(8,128)(2,1)S(1)}, bf16[2,2,256,256]{3,2,1,0:T(8,128)(2,1)}, u32[]{:S(2)}) copy-start(bf16[2,2,256,256]{3,2,1,0:T(8,128)(2,1)} %constant.32.clone.inner_ref) | copy-start | bytes 1572868
  97.1 23.7 %copy-start.3 = (f32[2,512,128]{2,1,0:T(8,128)S(1)}, f32[2,512,128]{2,1,0:T(8,128)}, u32[]{:S(2)}) copy-start(f32[2,512,128]{2,1,0:T(8,128)} %constant.33.clone.turn_ref) | copy-start | bytes 1572868
  97.1 23.7 %all-to-all-start.1 = ((f32[8,2,3,64,128]{4,3,2,1,0:T(8,128)}), f32[8,2,3,64,128]{4,3,2,1,0:T(8,128)S(1)}, u32[]{:S(2)}, u32[]{:S(2)}) async-start(f32[8,2,3,64,128]{4,3,2,1,0:T(8,128)} %shard_map.91), calls=%async_computation.1 | async-start | bytes 3145728 | tf_op jit(solution)/shard_map/all_to_all | solution.py:220
  120.8 2.2 copy-start
  123.0 1.6 copy-start.1
  241.5 6.5 %collective-permute-start = (f32[12,4,128]{2,1,0:T(4,128)S(1)}, f32[12,4,128]{2,1,0:T(4,128)S(1)}, u32[]{:S(2)}, u32[]{:S(2)}) collective-permute-start(f32[12,4,128]{2,1,0:T(4,128)S(1)} %get-tuple-element.11), channel_id=1, source_target_pairs={{0,1},{1,2},{2,3},{3,4},{4,5},{5,6},{6,7},{7,8},{8,9},{9,10},{10,1... | collective-permute-start | bytes 73736 | tf_op jit(solution)/shard_map/ppermute | solution.py:243
  243.4 6.0 %collective-permute-start.1 = (f32[12,4,128]{2,1,0:T(4,128)S(1)}, f32[12,4,128]{2,1,0:T(4,128)S(1)}, u32[]{:S(2)}, u32[]{:S(2)}) collective-permute-start(f32[12,4,128]{2,1,0:T(4,128)S(1)} %get-tuple-element.12), channel_id=1, source_target_pairs={{1,0},{2,1},{3,2},{4,3},{5,4},{6,5},{7,6},{8,7},{9,8},{10,9},{11,1... | collective-permute-start | bytes 73736 | tf_op jit(solution)/shard_map/ppermute | solution.py:244
  250.2 12.1 %copy-start.8 = (s32[96,96]{1,0:T(8,128)S(1)}, s32[96,96]{1,0:T(8,128)}, u32[]{:S(2)}) copy-start(s32[96,96]{1,0:T(8,128)} %param.12) | copy-start | bytes 110596
  254.1 8.4 %copy-start.7 = (s32[96,96]{1,0:T(8,128)S(1)}, s32[96,96]{1,0:T(8,128)}, u32[]{:S(2)}) copy-start(s32[96,96]{1,0:T(8,128)} %param.11) | copy-start | bytes 110596
  255.4 20.6 %all-to-all-start.4 = ((f32[8,12,15,128]{3,2,1,0:T(8,128)}), f32[8,12,15,128]{3,2,1,0:T(8,128)S(1)}, u32[]{:S(2)}, u32[]{:S(2)}) async-start(f32[8,12,15,128]{3,2,1,0:T(8,128)} %fusion.3), calls=%async_computation.4 | async-start | bytes 1572864 | tf_op jit(solution)/shard_map/all_to_all | solution.py:220
  276.0 0.9 copy-start.4
  282.3 13.5 %all-to-all-start.5 = ((f32[8,12,8,128]{3,2,1,0:T(8,128)}), f32[8,12,8,128]{3,2,1,0:T(8,128)S(1)}, u32[]{:S(2)}, u32[]{:S(2)}) async-start(f32[8,12,8,128]{3,2,1,0:T(8,128)} %bitcast.74), calls=%async_computation.5 | async-start | bytes 786432 | tf_op jit(solution)/shard_map/all_to_all | solution.py:220
  288.5 7.7 %copy-start.5 = (f32[2,8,64,128]{3,1,2,0:T(8,128)S(1)}, f32[2,8,64,128]{3,1,2,0:T(8,128)}, u32[]{:S(2)}) copy-start(f32[2,8,64,128]{3,1,2,0:T(8,128)} %copy.20) | copy-start | bytes 1572868
  298.2 1.1 copy-start.6

commit v2 on v1

v2 whole, which is shorter than its diff:
```python
import functools

import jax
import jax.numpy as jnp
import ml_dtypes
import numpy as np
from jax import lax
from jax.experimental import pallas as pl
from jax.experimental.pallas import tpu as pltpu
from jax.sharding import Mesh
from jax.sharding import PartitionSpec as P

HALO = 512
GAMMA_SELF = 0.1
GAMMA_CROSS = 0.05
SAMPLES = 524288
LANES = 128
COARSE = 8
FOLDED = SAMPLES // COARSE
OUTER = FOLDED // LANES
REACH = HALO // LANES
FIELD_ROWS = 2 * 3 * 64
SMEM = pltpu.SMEM
VMEM = pltpu.VMEM


def split_np(matrix):
    upper = matrix.astype(ml_dtypes.bfloat16)
    lower = (matrix - upper.astype(np.float64)).astype(ml_dtypes.bfloat16)
    return np.stack([upper, lower])


def roots(numerators, period):
    angles = (numerators % period) * (2.0 * np.pi / period)
    return np.cos(angles), np.sin(angles)


@functools.cache
def inner_table():
    lane_ids = np.arange(LANES, dtype=np.int64)
    cosine, sine = roots(lane_ids[:, None] * lane_ids[None, :], LANES)
    forward = np.block([[cosine, -sine], [sine, cosine]])
    return np.stack([split_np(forward), split_np(forward.T)])


@functools.cache
def tables():
    outer_ids = np.arange(OUTER, dtype=np.int64)
    lane_ids = np.arange(LANES, dtype=np.int64)
    residues = np.arange(COARSE, dtype=np.int64)
    half = OUTER // 2
    half_ids = np.arange(half, dtype=np.int64)
    cosine, sine = roots(half_ids[:, None] * half_ids[None, :], half)
    outer = np.stack([split_np(cosine), split_np(sine)])
    middle = np.stack(roots(half_ids[:, None] + 0 * lane_ids[None, :], OUTER))
    order = np.concatenate([outer_ids[0::2], outer_ids[1::2]])
    turn = np.stack(roots(order[:, None] * lane_ids[None, :], FOLDED))
    around = np.concatenate([outer_ids, np.arange(-REACH, 0), OUTER + np.arange(REACH)])
    time_ids = LANES * around[:, None] + lane_ids[None, :]
    shift = np.stack(roots(residues[:, None, None] * time_ids[None], SAMPLES), axis=1)
    freq_ids = residues[:, None, None] + COARSE * (
        order[None, :, None] + OUTER * lane_ids[None, None, :]
    )
    signed_ids = np.where(freq_ids < SAMPLES // 2, freq_ids, freq_ids - SAMPLES)
    response = np.stack(roots(signed_ids * signed_ids, 4 * SAMPLES), axis=1) / SAMPLES
    response = np.pad(response, ((0, 0), (0, 0), (0, 2 * REACH), (0, 0)))
    by_residue = np.concatenate([shift, response], axis=1).astype(np.float32)
    return outer, middle.astype(np.float32), turn.astype(np.float32), by_residue


def radix_eight(parts, sign):
    half = np.float32(np.sqrt(0.5))

    def add(a, b):
        return a[0] + b[0], a[1] + b[1]

    def sub(a, b):
        return a[0] - b[0], a[1] - b[1]

    def quarter(a):
        return (-sign * a[1], sign * a[0])

    def eighth(a):
        return (half * (a[0] - sign * a[1]), half * (a[1] + sign * a[0]))

    def four(a, b, c, d):
        even_sum, even_diff = add(a, c), sub(a, c)
        odd_sum, odd_diff = add(b, d), quarter(sub(b, d))
        return (
            add(even_sum, odd_sum),
            add(even_diff, odd_diff),
            sub(even_sum, odd_sum),
            sub(even_diff, odd_diff),
        )

    even = four(*(add(parts[i], parts[i + 4]) for i in range(4)))
    diffs = [sub(parts[i], parts[i + 4]) for i in range(4)]
    odd = four(
        diffs[0], eighth(diffs[1]), quarter(diffs[2]), quarter(eighth(diffs[3]))
    )
    return [pair for both in zip(even, odd) for pair in both]


def head_kernel(in_ref, out_ref):
    for group in range(COARSE):
        for row in range(3):
            chan, pol = divmod(3 * group + row, 2)
            for part in range(2):
                out_ref[group, part, row] = in_ref[part, chan, pl.ds(pol, 64, stride=2), :]


def head(launched):
    vmem = pl.BlockSpec(memory_space=VMEM)
    return pl.pallas_call(
        head_kernel,
        in_specs=[vmem],
        out_specs=vmem,
        out_shape=jax.ShapeDtypeStruct((COARSE, 2, 3, 64, LANES), jnp.float32),
        name="head",
    )(interleaved(launched))


def interleaved(values):
    lead = values.shape[:-2]
    blocks = values.shape[-1] // LANES
    values = values.reshape(lead + (2, blocks, LANES))
    return jnp.swapaxes(values, -3, -2).reshape(lead + (2 * blocks, LANES))


def fold_kernel(in_ref, out_ref):
    rows = 8
    for row in range(in_ref.shape[2]):
        for step in range(in_ref.shape[3] // rows):
            at = slice(step * rows, step * rows + rows)
            parts = [(in_ref[i, 0, row, at, :], in_ref[i, 1, row, at, :]) for i in range(COARSE)]
            for i, pair in enumerate(radix_eight(parts, -1)):
                out_ref[i, 0, row, at, :] = pair[0]
                out_ref[i, 1, row, at, :] = pair[1]


def fold(values):
    spec = pl.BlockSpec((COARSE, 2, 3, 32, LANES), lambda k: (0, 0, 0, k, 0))
    return pl.pallas_call(
        fold_kernel,
        grid=(2,),
        in_specs=[spec],
        out_specs=spec,
        out_shape=jax.ShapeDtypeStruct(values.shape, jnp.float32),
        name="fold",
    )(values)


def halves(values):
    upper = values.astype(jnp.bfloat16)
    lower = (values - upper.astype(jnp.float32)).astype(jnp.bfloat16)
    return upper, lower


def dot(left, right):
    return jnp.dot(left, right, preferred_element_type=jnp.float32)


def triple(left, right):
    return dot(left[0], right[0]) + (dot(left[0], right[1]) + dot(left[1], right[0]))


def turned(real, imag, cosine, sine, sign):
    if sign > 0:
        return real * cosine - imag * sine, imag * cosine + real * sine
    return real * cosine + imag * sine, imag * cosine - real * sine


def packed(real, imag):
    return halves(jnp.concatenate([real, imag], axis=1))


def outer_dft(outer_ref, first, second, sign):
    values = halves(jnp.concatenate([*first, *second], axis=1))
    by_cos = triple((outer_ref[0, 0], outer_ref[0, 1]), values)
    by_sin = triple((outer_ref[1, 0], outer_ref[1, 1]), values)
    found = []
    for low in (0, 2 * LANES):
        cos_real, cos_imag = by_cos[:, low : low + LANES], by_cos[:, low + LANES : low + 2 * LANES]
        sin_real, sin_imag = by_sin[:, low : low + LANES], by_sin[:, low + LANES : low + 2 * LANES]
        if sign > 0:
            found.append((cos_real - sin_imag, cos_imag + sin_real))
        else:
            found.append((cos_real + sin_imag, cos_imag - sin_real))
    return found


def disperse_kernel(in_ref, outer_ref, inner_ref, middle_ref, turn_ref, own_ref, out_ref, work):
    half = OUTER // 2
    middle = (middle_ref[0], middle_ref[1])
    for row in range(in_ref.shape[2]):
        real = in_ref[:, 0, row].reshape(OUTER, LANES)
        imag = in_ref[:, 1, row].reshape(OUTER, LANES)
        real, imag = turned(real, imag, own_ref[0, :OUTER], own_ref[1, :OUTER], -1)
        even = (real[:half] + real[half:], imag[:half] + imag[half:])
        odd = turned(real[:half] - real[half:], imag[:half] - imag[half:], *middle, -1)
        even, odd = outer_dft(outer_ref, even, odd, -1)
        real, imag = (jnp.concatenate([even[k], odd[k]], axis=0) for k in range(2))
        values = packed(*turned(real, imag, turn_ref[0], turn_ref[1], -1))
        both = triple(values, (inner_ref[0, 0], inner_ref[0, 1]))
        real, imag = turned(
            both[:, :LANES], both[:, LANES:], own_ref[2, :OUTER], own_ref[3, :OUTER], 1
        )
        both = triple(packed(real, imag), (inner_ref[1, 0], inner_ref[1, 1]))
        real, imag = turned(both[:, :LANES], both[:, LANES:], turn_ref[0], turn_ref[1], 1)
        even, odd = outer_dft(
            outer_ref, (real[:half], imag[:half]), (real[half:], imag[half:]), 1
        )
        odd = turned(*odd, *middle, 1)
        for part in range(2):
            work[part, :half] = even[part] + odd[part]
            work[part, half:OUTER] = even[part] - odd[part]
            work[part, OUTER : OUTER + REACH] = work[part, OUTER - REACH : OUTER]
            work[part, OUTER + REACH :] = work[part, :REACH]
        work[0], work[1] = turned(work[0], work[1], own_ref[0], own_ref[1], 1)
        for group in range(8):
            low, high = 64 * group, 64 * group + 64
            before = low - REACH if group else OUTER
            after = high if group < 7 else OUTER + REACH
            for part in range(2):
                out_ref[group, part, row, :64] = work[part, low:high]
                out_ref[group, part, row, 64 : 64 + REACH] = work[part, before : before + REACH]
                out_ref[group, part, row, 64 + REACH :] = work[part, after : after + REACH]


def disperse(values, own):
    outer, middle, turn, _ = tables()
    vmem = pl.BlockSpec(memory_space=VMEM)
    shape = values.shape[:3] + (64 + 2 * REACH, LANES)
    return pl.pallas_call(
        disperse_kernel,
        in_specs=[vmem] * 6,
        out_specs=vmem,
        out_shape=jax.ShapeDtypeStruct(shape, jnp.float32),
        scratch_shapes=[VMEM((2, OUTER + 2 * REACH, LANES), jnp.float32)],
        compiler_params=pltpu.CompilerParams(vmem_limit_bytes=32 * 1024 * 1024),
        name="disperse",
    )(values, outer, inner_table(), middle, turn, own)


def field_rows(part, row):
    low = (3 * part + row) * 64
    return slice(low, low + 64)


def unfold_kernel(place_ref, in_ref, out_ref):
    rows = 8
    even = place_ref[0] % 2 == 0
    for step in range(in_ref.shape[3] // rows):
        at = slice(step * rows, step * rows + rows)
        squares = []
        for row in range(3):
            parts = [(in_ref[i, 0, row, at, :], in_ref[i, 1, row, at, :]) for i in range(COARSE)]
            results = radix_eight(parts, 1)
            if step < 8:
                for i, pair in enumerate(results):
                    for part in range(2):
                        low = field_rows(part, row).start + step * rows
                        out_ref[i, low : low + rows, :] = pair[part]
            else:
                squares.append([real * real + imag * imag for real, imag in results])
        if step == 8:
            for i in range(COARSE):
                middle = squares[1][i]
                nothing = jnp.zeros_like(middle)
                first = squares[0][i] + jnp.where(even, middle, nothing)
                second = squares[2][i] + jnp.where(even, nothing, middle)
                out_ref[i, FIELD_ROWS : FIELD_ROWS + rows, :] = first
                out_ref[i, FIELD_ROWS + rows :, :] = second


def unfold(values, place):
    vmem = pl.BlockSpec(memory_space=VMEM)
    shape = (COARSE, FIELD_ROWS + 16, LANES)
    return pl.pallas_call(
        unfold_kernel,
        in_specs=[pl.BlockSpec(memory_space=SMEM), vmem],
        out_specs=vmem,
        out_shape=jax.ShapeDtypeStruct(shape, jnp.float32),
        compiler_params=pltpu.CompilerParams(vmem_limit_bytes=24 * 1024 * 1024),
        name="unfold",
    )(place, values)


def fields_of(held, chan):
    found = []
    for pol in range(2):
        group, row = divmod(2 * chan + pol, 3)
        found.append((held[group, field_rows(0, row), :], held[group, field_rows(1, row), :]))
    return found


def slide_kernel(held, table_ref, out_ref, extended):
    groups, local_chan, taken, _ = out_ref.shape
    table = table_ref[...]
    span = 64 + 2 * REACH
    for chan in range(local_chan):
        powers = sum(real * real + imag * imag for real, imag in fields_of(held, chan))
        extended[chan, REACH : REACH + 64, :] = powers
        pair, place = divmod(chan, 3)
        low = FIELD_ROWS + (place + 1) // 2 * 8
        around = held[2 * pair + place // 2, low : low + 8, :]
        if place == 1:
            around = around + held[2 * pair + 1, FIELD_ROWS : FIELD_ROWS + 8, :]
        extended[chan, :REACH, :] = around[:REACH]
        extended[chan, 64 + REACH : span, :] = around[REACH:]
        extended[chan, span:, :] = jnp.zeros_like(around)
        both = jnp.concatenate(
            [extended[chan, :span, :], extended[chan, 1 : span + 1, :]], axis=1
        )
        upper, lower = halves(both)
        sliding = dot(upper, table) + dot(lower, table)
        for group in range(groups):
            out_ref[group, chan] = sliding[8 * group : 8 * group + taken]


def slide(fields, groups, local_chan):
    rows_idx = np.arange(2 * LANES)[:, None]
    cols_idx = np.arange(LANES)[None, :]
    table = ((rows_idx >= cols_idx) & (rows_idx < cols_idx + LANES)).astype(ml_dtypes.bfloat16)
    vmem = pl.BlockSpec(memory_space=VMEM)
    return pl.pallas_call(
        slide_kernel,
        in_specs=[vmem, vmem],
        out_specs=vmem,
        out_shape=jax.ShapeDtypeStruct((groups, local_chan, 16, LANES), jnp.float32),
        scratch_shapes=[VMEM((local_chan, 64 + 2 * REACH + 8, LANES), jnp.float32)],
        compiler_params=pltpu.CompilerParams(vmem_limit_bytes=24 * 1024 * 1024),
        name="slide",
    )(fields, table)


def cross_kernel(starts_ref, lengths_ref, in_ref, out_ref, gathered, weights, uppers, lowers):
    channels = starts_ref.shape[0]
    shifts = weights.shape[2] // LANES
    own = out_ref.shape[1]
    taken = in_ref.shape[0] // channels
    starts, lengths = starts_ref[...], lengths_ref[...]
    inverse = 1.0 / lengths.astype(jnp.float32)
    others = lax.broadcasted_iota(jnp.int32, starts.shape, 0) != lax.broadcasted_iota(
        jnp.int32, starts.shape, 1
    )
    nothing = jnp.zeros_like(inverse)
    weights[...] = jnp.zeros_like(weights)
    for shift in range(shifts):
        offset = LANES * shift - HALO
        inside = (starts <= offset) & (offset + LANES <= starts + lengths)
        values = halves(jnp.where(inside & others, inverse, nothing))
        for k in range(2):
            weights[k, :, shift * LANES : shift * LANES + channels] = values[k]
    gathered[...] = jnp.zeros_like(gathered)
    for step in range(taken - 1):
        gathered[:channels, :] = in_ref[pl.ds(step, channels, stride=taken), :]
        at = slice(step * LANES, (step + 1) * LANES)
        uppers[at, :], lowers[at, :] = halves(gathered[...])
    pair_weights = (weights[0], weights[1])
    for step in range(0, own, 2):

        def pair(ref):
            low, depth = step * LANES, shifts * LANES
            return jnp.concatenate(
                [ref[low : low + depth, :], ref[low + LANES : low + LANES + depth, :]], axis=1
            )

        both = triple(pair_weights, (pair(uppers), pair(lowers)))
        out_ref[:, step, :] = both[:, :LANES]
        out_ref[:, step + 1, :] = both[:, LANES:]


def cross(starts, lengths, blocks, own):
    channels = starts.shape[0]
    shifts = 2 * HALO // LANES
    taken = blocks.shape[2]
    vmem = pl.BlockSpec(memory_space=VMEM)
    return pl.pallas_call(
        cross_kernel,
        in_specs=[vmem] * 3,
        out_specs=vmem,
        out_shape=jax.ShapeDtypeStruct((channels, own, LANES), jnp.float32),
        scratch_shapes=[
            VMEM((LANES, LANES), jnp.float32),
            VMEM((2, channels, shifts * LANES), jnp.bfloat16),
            VMEM(((taken - 1) * LANES, LANES), jnp.bfloat16),
            VMEM(((taken - 1) * LANES, LANES), jnp.bfloat16),
        ],
        name="cross",
    )(starts, lengths, blocks.reshape(-1, LANES))


def cosine_and_sine(angles):
    turns = jnp.floor(angles * np.float32(2.0 / np.pi) + 0.5)
    rest = ((angles - turns * 1.5703125) - turns * 4.837512969970703125e-4) - turns * np.float32(
        7.54978995489188216e-8
    )
    square = rest * rest
    sine = rest + rest * square * (
        -1.6666654611e-1 + square * (8.3321608736e-3 + square * -1.9515295891e-4)
    )
    cosine = (1.0 - 0.5 * square) + square * square * (
        4.166664568298827e-2 + square * (-1.388731625493765e-3 + square * 2.443315711809948e-5)
    )
    quadrant = turns.astype(jnp.int32) & 3
    swap = (quadrant & 1) == 1
    near, far = jnp.where(swap, sine, cosine), jnp.where(swap, cosine, sine)
    turned = (quadrant == 1) | (quadrant == 2)
    return jnp.where(turned, -near, near), jnp.where(quadrant >= 2, -far, far)


def tail_kernel(held, cross_ref, noise_ref, out_ref):
    for chan in range(out_ref.shape[1]):
        fields = fields_of(held, chan)
        others = cross_ref[:, chan].reshape(64, LANES)
        powers = sum(real * real + imag * imag for real, imag in fields)
        cosine, sine = cosine_and_sine(GAMMA_SELF * powers + GAMMA_CROSS * others)
        for pol, (real, imag) in enumerate(fields):
            at = pl.ds(pol, 64, stride=2)
            out_ref[0, chan, at, :] = cosine * real - sine * imag
            out_ref[1, chan, at, :] = cosine * imag + sine * real
        for part in range(2):
            out_ref[part, chan] = out_ref[part, chan] + noise_ref[part, chan].astype(jnp.float32)


def tail(fields, cross_sum, amp_noise):
    local_chan = cross_sum.shape[1]
    vmem = pl.BlockSpec(memory_space=VMEM)
    received = pl.pallas_call(
        tail_kernel,
        in_specs=[vmem] * 3,
        out_specs=vmem,
        out_shape=jax.ShapeDtypeStruct((2, local_chan, 128, LANES), jnp.float32),
        compiler_params=pltpu.CompilerParams(vmem_limit_bytes=24 * 1024 * 1024),
        name="tail",
    )(fields, cross_sum, interleaved(amp_noise))
    received = received.reshape(2, local_chan, 64, 2, LANES)
    return jnp.swapaxes(received, 2, 3).reshape(amp_noise.shape)


def exchange(values, axis):
    return lax.all_to_all(values, axis, 0, 0, tiled=True)


def per_device(launched, amp_noise, window_start, window_length):
    local_chan = launched.shape[1]
    groups = lax.axis_size("chan")
    place = lax.axis_index("j").astype(jnp.int32).reshape(1)
    own_tables = lax.dynamic_index_in_dim(
        jnp.asarray(tables()[3]), lax.axis_index("i"), 0, keepdims=False
    )
    values = exchange(head(launched), "j")
    values = exchange(fold(values), "i")
    values = exchange(disperse(values, own_tables), "i")
    fields = exchange(unfold(values, place), "j")
    blocks = exchange(slide(fields, groups, local_chan), "chan")
    cross_sum = cross(window_start, window_length, blocks, 64 // groups)
    cross_sum = exchange(cross_sum.reshape(groups, local_chan, -1, LANES), "chan")
    return tail(fields, cross_sum, amp_noise)


def solution(mesh):
    split = Mesh(mesh.devices.reshape(mesh.shape["chan"], COARSE, -1), ("chan", "j", "i"))
    fields = P(None, "chan", None, ("j", "i"))
    return jax.shard_map(
        per_device,
        mesh=split,
        in_specs=(fields, fields, P(), P()),
        out_specs=fields,
        check_vma=False,
    )
```

time: 303 us -> 278 us (0.917)
  local copies, waits for them, and re-layouts: 20 us -> 3.49 us
  starting transfers between devices: 21.1 us -> 7.17 us
  blocking collectives: 194 us -> 207 us
  other arithmetic: 7.6 us -> 0 us
    all_to_all x3 -> x4, blocking collectives: 194 us -> 207 us  [exchange(): return lax.all_to_all(values, axis, 0, 0, tiled=True)]
    unnamed x29 -> x12, local copies, waits for them, and re-layouts: 10.8 us -> 2.11 us
    all_to_all x3 -> x2, starting transfers between devices: 14.6 us -> 7.17 us  [exchange(): return lax.all_to_all(values, axis, 0, 0, tiled=True)]
    ppermute x2 -> x0, starting transfers between devices: 6.46 us -> none  [the longest x1 4.54 us: per_device(): after = lax.ppermute(powers[:, :reach], ('j', 'i'), down)]
    all_to_all x3 -> x2, waiting for transfers between devices: 36.5 us -> 40.7 us  [exchange(): return lax.all_to_all(values, axis, 0, 0, tiled=True)]
    reshape x3 -> x0, local copies, waits for them, and re-layouts: 3.66 us -> none  [the longest x2 2.73 us: per_device(): launched.reshape(2, COARSE, rows // COARSE, blocks, LANES)]
    pallas_call x4 -> x7, Pallas kernels: 19.6 us -> 18.3 us  [the longest x1 6.97 us: disperse(): pl.pallas_call(disperse_kernel, in_specs=[vmem] * 6, out_specs=vmem, out_...]
  transfers between devices with their start and end apart: 5 -> 2, of which waited for: 4 -> 2; matrix products, arithmetic and copies ran while one was open for 2% -> 0% of each run, Pallas kernels for 0% -> 0%
where the time goes in v2:
time: 278 us; the launch traced here: 277 us
  blocking collectives  207 us (74%)
  waiting for transfers between devices  40.7 us (15%)
  Pallas kernels  18.3 us (7%)
  starting transfers between devices  7.17 us (3%)
  local copies, waits for them, and re-layouts  3.49 us (1%)
    all_to_all x4, blocking collectives, exchange(): return lax.all_to_all(values, axis, 0, 0, tiled=True)  207 us
    all_to_all x2, waiting for transfers between devices, exchange(): return lax.all_to_all(values, axis, 0, 0, tiled=True)  40.7 us
    all_to_all x2, starting transfers between devices, exchange(): return lax.all_to_all(values, axis, 0, 0, tiled=True)  7.17 us
    pallas_call x1, Pallas kernels, disperse(): pl.pallas_call(disperse_kernel, in_specs=[vmem] * 6, out_specs=vmem, out_...  6.97 us
  transfers between devices with their start and end apart: 2, of which 2 were waited for; matrix products, arithmetic and copies ran while one was open for 0% of the time, Pallas kernels for 0%

profile of v2, /device:TPU:64, one launch (start us, length us, event | category | flops | bytes accessed | tf_op | source)
XLA Modules:
  0.0 277.0 jit_solution(18294569266512122795)
XLA Ops:
  0.0 2.7 head.1
  2.7 90.9 %all_to_all.30.in_ref = f32[8,2,3,64,128]{4,3,2,1,0:T(8,128)} all-to-all(f32[8,2,3,64,128]{4,3,2,1,0:T(8,128)} %head.1), channel_id=1, replica_groups=mesh['chan'=8,'j'=8,'i'=8] {'j'}, dimensions={0} | all-to-all | bytes 3145728 | tf_op jit(solution)/shard_map/all_to_all | solution.py:443
  93.6 2.4 fold.1
  96.0 3.6 %all-to-all-start.1 = ((f32[8,2,3,64,128]{4,3,2,1,0:T(8,128)}), f32[8,2,3,64,128]{4,3,2,1,0:T(8,128)S(1)}, u32[]{:S(2)}, u32[]{:S(2)}) async-start(f32[8,2,3,64,128]{4,3,2,1,0:T(8,128)} %fold.1), calls=%async_computation.1 | async-start | bytes 3145728 | tf_op jit(solution)/shard_map/all_to_all | solution.py:443
  99.6 0.0 copy-start.1
  99.6 0.0 copy-start.4
  99.6 1.4 dynamic-slice_bitcast_fusion.own_ref
  101.0 18.6 %all-to-all-done.1.in_ref = f32[8,2,3,64,128]{4,3,2,1,0:T(8,128)S(1)} async-done(((f32[8,2,3,64,128]{4,3,2,1,0:T(8,128)}), f32[8,2,3,64,128]{4,3,2,1,0:T(8,128)S(1)}, u32[]{:S(2)}, u32[]{:S(2)}) %all-to-all-start.1) | async-done | bytes 1572896 | tf_op jit(solution)/shard_map/all_to_all | solution.py:443
  119.6 0.0 copy-done.1
  119.6 1.0 copy-done.2
  120.6 1.0 copy-done.3
  121.7 7.0 %disperse.1 = f32[8,2,3,72,128]{4,3,2,1,0:T(8,128)} custom-call(f32[8,2,3,64,128]{4,3,2,1,0:T(8,128)S(1)} %all-to-all-done.1.in_ref, bf16[2,2,256,256]{3,2,1,0:T(8,128)(2,1)S(1)} %copy-done.3, bf16[2,2,256,256]{3,2,1,0:T(8,128)(2,1)S(1)} %copy-done.2, f32[2,256,128]{2,1,0:T(8,128)S(1)} %copy-done.4, f32[2,512,128]{2,1,0:T(8,128)S(1)} %copy-done.1, ...), custom_call_target="tpu_custom_call" | custom-call | tf_op jit(solution)/shard_map/disperse/pallas_call | solution.py:234
  128.7 3.6 %all-to-all-start.2 = ((f32[8,2,3,72,128]{4,3,2,1,0:T(8,128)}), f32[8,2,3,72,128]{4,3,2,1,0:T(8,128)S(1)}, u32[]{:S(2)}, u32[]{:S(2)}) async-start(f32[8,2,3,72,128]{4,3,2,1,0:T(8,128)} %disperse.1), calls=%async_computation.2 | async-start | bytes 3538944 | tf_op jit(solution)/shard_map/all_to_all | solution.py:443
  132.3 22.1 %all-to-all-done.2.in_ref = f32[8,2,3,72,128]{4,3,2,1,0:T(8,128)S(1)} async-done(((f32[8,2,3,72,128]{4,3,2,1,0:T(8,128)}), f32[8,2,3,72,128]{4,3,2,1,0:T(8,128)S(1)}, u32[]{:S(2)}, u32[]{:S(2)}) %all-to-all-start.2) | async-done | bytes 1769504 | tf_op jit(solution)/shard_map/all_to_all | solution.py:443
  154.4 0.3 unfold.1
  154.6 0.0 copy-start.5
  154.6 82.9 %all_to_all.31.held = f32[8,400,128]{2,1,0:T(8,128)S(1)} all-to-all(f32[8,400,128]{2,1,0:T(8,128)S(1)} %unfold.1), channel_id=1, replica_groups=mesh['chan'=8,'j'=8,'i'=8] {'j'}, dimensions={0} | all-to-all | bytes 3276800 | tf_op jit(solution)/shard_map/all_to_all | solution.py:443
  237.5 0.4 slide.1
  238.0 0.0 copy-start
  238.0 20.7 %all_to_all.32 = f32[8,12,16,128]{3,2,1,0:T(8,128)} all-to-all(f32[8,12,16,128]{3,2,1,0:T(8,128)S(1)} %slide.1), channel_id=1, replica_groups=mesh['chan'=8,'j'=8,'i'=8] {'chan'}, dimensions={0} | all-to-all | bytes 1572864 | tf_op jit(solution)/shard_map/all_to_all | solution.py:443
  258.7 3.5 %cross.1 = f32[96,8,128]{2,1,0:T(8,128)} custom-call(s32[96,96]{1,0:T(8,128)} %starts_ref.1, s32[96,96]{1,0:T(8,128)} %lengths_ref.1, f32[1536,128]{1,0:T(8,128)} %bitcast.21), custom_call_target="tpu_custom_call" | custom-call | tf_op jit(solution)/shard_map/cross/pallas_call | solution.py:379
  262.2 12.7 %all_to_all.33.cross_ref = f32[8,12,8,128]{3,2,1,0:T(8,128)S(1)} all-to-all(f32[8,12,8,128]{3,2,1,0:T(8,128)} %bitcast.23), channel_id=1, replica_groups=mesh['chan'=8,'j'=8,'i'=8] {'chan'}, dimensions={0} | all-to-all | bytes 786432 | tf_op jit(solution)/shard_map/all_to_all | solution.py:443
  274.8 0.0 copy-done
  274.8 2.1 tail.1
  (4 shorter events, 0.0 us)
Async XLA Ops:
  96.0 23.6 %all-to-all-start.1 = ((f32[8,2,3,64,128]{4,3,2,1,0:T(8,128)}), f32[8,2,3,64,128]{4,3,2,1,0:T(8,128)S(1)}, u32[]{:S(2)}, u32[]{:S(2)}) async-start(f32[8,2,3,64,128]{4,3,2,1,0:T(8,128)} %fold.1), calls=%async_computation.1 | async-start | bytes 3145728 | tf_op jit(solution)/shard_map/all_to_all | solution.py:443
  99.6 20.0 %copy-start.1 = (f32[2,512,128]{2,1,0:T(8,128)S(1)}, f32[2,512,128]{2,1,0:T(8,128)}, u32[]{:S(2)}) copy-start(f32[2,512,128]{2,1,0:T(8,128)} %constant.29.clone.turn_ref) | copy-start | bytes 1572868
  99.6 20.0 %copy-start.4 = (f32[2,256,128]{2,1,0:T(8,128)S(1)}, f32[2,256,128]{2,1,0:T(8,128)}, u32[]{:S(2)}) copy-start(f32[2,256,128]{2,1,0:T(8,128)} %constant.28.clone.middle_ref) | copy-start | bytes 786436
  119.6 1.0 copy-start.2
  120.6 1.0 copy-start.3
  128.7 25.7 %all-to-all-start.2 = ((f32[8,2,3,72,128]{4,3,2,1,0:T(8,128)}), f32[8,2,3,72,128]{4,3,2,1,0:T(8,128)S(1)}, u32[]{:S(2)}, u32[]{:S(2)}) async-start(f32[8,2,3,72,128]{4,3,2,1,0:T(8,128)} %disperse.1), calls=%async_computation.2 | async-start | bytes 3538944 | tf_op jit(solution)/shard_map/all_to_all | solution.py:443
  154.6 82.9 %copy-start.5 = (bf16[256,128]{1,0:T(8,128)(2,1)S(1)}, bf16[256,128]{1,0:T(8,128)(2,1)}, u32[]{:S(2)}) copy-start(bf16[256,128]{1,0:T(8,128)(2,1)} %constant.30.clone.table_ref) | copy-start | bytes 196612
  238.0 36.9 %copy-start = (bf16[2,12,2,8192]{3,2,1,0:T(2,128)(2,1)S(1)}, bf16[2,12,2,8192]{3,2,1,0:T(2,128)(2,1)}, u32[]{:S(2)}) copy-start(bf16[2,12,2,8192]{3,2,1,0:T(2,128)(2,1)} %param.11) | copy-start | bytes 2359300

commit v3 on v2

--- a/solution.py
+++ b/solution.py
@@ -19,6 +19,7 @@
 FOLDED = SAMPLES // COARSE
 OUTER = FOLDED // LANES
 REACH = HALO // LANES
+WHOLE = 8
 FIELD_ROWS = 2 * 3 * 64
 SMEM = pltpu.SMEM
 VMEM = pltpu.VMEM
@@ -101,10 +102,13 @@
     return [pair for both in zip(even, odd) for pair in both]
 
 
+def rows_of(group):
+    return ((group, 0), (group, 1), (WHOLE + group // 2, group % 2))
+
+
 def head_kernel(in_ref, out_ref):
     for group in range(COARSE):
-        for row in range(3):
-            chan, pol = divmod(3 * group + row, 2)
+        for row, (chan, pol) in enumerate(rows_of(group)):
             for part in range(2):
                 out_ref[group, part, row] = in_ref[part, chan, pl.ds(pol, 64, stride=2), :]
 
@@ -174,10 +178,10 @@
     return halves(jnp.concatenate([real, imag], axis=1))
 
 
-def outer_dft(outer_ref, first, second, sign):
+def outer_dft(dft_ref, first, second, sign):
     values = halves(jnp.concatenate([*first, *second], axis=1))
-    by_cos = triple((outer_ref[0, 0], outer_ref[0, 1]), values)
-    by_sin = triple((outer_ref[1, 0], outer_ref[1, 1]), values)
+    by_cos = triple((dft_ref[0, 0], dft_ref[0, 1]), values)
+    by_sin = triple((dft_ref[1, 0], dft_ref[1, 1]), values)
     found = []
     for low in (0, 2 * LANES):
         cos_real, cos_imag = by_cos[:, low : low + LANES], by_cos[:, low + LANES : low + 2 * LANES]
@@ -189,7 +193,7 @@
     return found
 
 
-def disperse_kernel(in_ref, outer_ref, inner_ref, middle_ref, turn_ref, own_ref, out_ref, work):
+def disperse_kernel(in_ref, dft_ref, middle_ref, turn_ref, own_ref, out_ref, work):
     half = OUTER // 2
     middle = (middle_ref[0], middle_ref[1])
     for row in range(in_ref.shape[2]):
@@ -198,17 +202,17 @@
         real, imag = turned(real, imag, own_ref[0, :OUTER], own_ref[1, :OUTER], -1)
         even = (real[:half] + real[half:], imag[:half] + imag[half:])
         odd = turned(real[:half] - real[half:], imag[:half] - imag[half:], *middle, -1)
-        even, odd = outer_dft(outer_ref, even, odd, -1)
+        even, odd = outer_dft(dft_ref, even, odd, -1)
         real, imag = (jnp.concatenate([even[k], odd[k]], axis=0) for k in range(2))
         values = packed(*turned(real, imag, turn_ref[0], turn_ref[1], -1))
-        both = triple(values, (inner_ref[0, 0], inner_ref[0, 1]))
+        both = triple(values, (dft_ref[2, 0], dft_ref[2, 1]))
         real, imag = turned(
             both[:, :LANES], both[:, LANES:], own_ref[2, :OUTER], own_ref[3, :OUTER], 1
         )
-        both = triple(packed(real, imag), (inner_ref[1, 0], inner_ref[1, 1]))
+        both = triple(packed(real, imag), (dft_ref[3, 0], dft_ref[3, 1]))
         real, imag = turned(both[:, :LANES], both[:, LANES:], turn_ref[0], turn_ref[1], 1)
         even, odd = outer_dft(
-            outer_ref, (real[:half], imag[:half]), (real[half:], imag[half:]), 1
+            dft_ref, (real[:half], imag[:half]), (real[half:], imag[half:]), 1
         )
         odd = turned(*odd, *middle, 1)
         for part in range(2):
@@ -233,13 +237,13 @@
     shape = values.shape[:3] + (64 + 2 * REACH, LANES)
     return pl.pallas_call(
         disperse_kernel,
-        in_specs=[vmem] * 6,
+        in_specs=[vmem] * 5,
         out_specs=vmem,
         out_shape=jax.ShapeDtypeStruct(shape, jnp.float32),
         scratch_shapes=[VMEM((2, OUTER + 2 * REACH, LANES), jnp.float32)],
         compiler_params=pltpu.CompilerParams(vmem_limit_bytes=32 * 1024 * 1024),
         name="disperse",
-    )(values, outer, inner_table(), middle, turn, own)
+    )(values, np.concatenate([outer, inner_table()]), middle, turn, own)
 
 
 def field_rows(part, row):
@@ -247,9 +251,8 @@
     return slice(low, low + 64)
 
 
-def unfold_kernel(place_ref, in_ref, out_ref):
+def unfold_kernel(in_ref, out_ref):
     rows = 8
-    even = place_ref[0] % 2 == 0
     for step in range(in_ref.shape[3] // rows):
         at = slice(step * rows, step * rows + rows)
         squares = []
@@ -265,63 +268,70 @@
                 squares.append([real * real + imag * imag for real, imag in results])
         if step == 8:
             for i in range(COARSE):
-                middle = squares[1][i]
-                nothing = jnp.zeros_like(middle)
-                first = squares[0][i] + jnp.where(even, middle, nothing)
-                second = squares[2][i] + jnp.where(even, nothing, middle)
-                out_ref[i, FIELD_ROWS : FIELD_ROWS + rows, :] = first
-                out_ref[i, FIELD_ROWS + rows :, :] = second
-
-
-def unfold(values, place):
-    vmem = pl.BlockSpec(memory_space=VMEM)
-    shape = (COARSE, FIELD_ROWS + 16, LANES)
+                out_ref[i, FIELD_ROWS : FIELD_ROWS + rows, :] = squares[0][i] + squares[1][i]
+                out_ref[i, FIELD_ROWS + rows :, :] = squares[2][i]
+
+
+def unfold(values):
+    vmem = pl.BlockSpec(memory_space=VMEM)
     return pl.pallas_call(
         unfold_kernel,
-        in_specs=[pl.BlockSpec(memory_space=SMEM), vmem],
-        out_specs=vmem,
-        out_shape=jax.ShapeDtypeStruct(shape, jnp.float32),
+        in_specs=[vmem],
+        out_specs=vmem,
+        out_shape=jax.ShapeDtypeStruct((COARSE, FIELD_ROWS + 4 * REACH, LANES), jnp.float32),
         compiler_params=pltpu.CompilerParams(vmem_limit_bytes=24 * 1024 * 1024),
         name="unfold",
-    )(place, values)
+    )(values)
 
 
 def fields_of(held, chan):
     found = []
     for pol in range(2):
-        group, row = divmod(2 * chan + pol, 3)
+        group, row = (chan, pol) if chan < WHOLE else (2 * (chan - WHOLE) + pol, 2)
         found.append((held[group, field_rows(0, row), :], held[group, field_rows(1, row), :]))
     return found
+
+
+def powers_around(held, chan):
+    if chan < WHOLE:
+        return held[chan, FIELD_ROWS : FIELD_ROWS + 2 * REACH, :]
+    group = 2 * (chan - WHOLE)
+    return held[group, FIELD_ROWS + 2 * REACH :, :] + held[group + 1, FIELD_ROWS + 2 * REACH :, :]
+
+
+def sliding_sums(powers, around, table, extended):
+    span = 64 + 2 * REACH
+    extended[REACH : REACH + 64, :] = powers
+    extended[:REACH, :] = around[:REACH]
+    extended[64 + REACH : span, :] = around[REACH:]
+    extended[span:, :] = jnp.zeros_like(around)
+    both = jnp.concatenate([extended[:span, :], extended[1 : span + 1, :]], axis=1)
+    upper, lower = halves(both)
+    return dot(upper, table) + dot(lower, table)
+
+
+def total(fields):
+    return sum(real * real + imag * imag for real, imag in fields)
 
 
 def slide_kernel(held, table_ref, out_ref, extended):
     groups, local_chan, taken, _ = out_ref.shape
     table = table_ref[...]
-    span = 64 + 2 * REACH
     for chan in range(local_chan):
-        powers = sum(real * real + imag * imag for real, imag in fields_of(held, chan))
-        extended[chan, REACH : REACH + 64, :] = powers
-        pair, place = divmod(chan, 3)
-        low = FIELD_ROWS + (place + 1) // 2 * 8
-        around = held[2 * pair + place // 2, low : low + 8, :]
-        if place == 1:
-            around = around + held[2 * pair + 1, FIELD_ROWS : FIELD_ROWS + 8, :]
-        extended[chan, :REACH, :] = around[:REACH]
-        extended[chan, 64 + REACH : span, :] = around[REACH:]
-        extended[chan, span:, :] = jnp.zeros_like(around)
-        both = jnp.concatenate(
-            [extended[chan, :span, :], extended[chan, 1 : span + 1, :]], axis=1
-        )
-        upper, lower = halves(both)
-        sliding = dot(upper, table) + dot(lower, table)
+        powers = total(fields_of(held, chan))
+        around = powers_around(held, chan)
+        sliding = sliding_sums(powers, around, table, extended.at[chan])
         for group in range(groups):
             out_ref[group, chan] = sliding[8 * group : 8 * group + taken]
 
 
-def slide(fields, groups, local_chan):
+def slide_table():
     rows_idx = np.arange(2 * LANES)[:, None]
     cols_idx = np.arange(LANES)[None, :]
-    table = ((rows_idx >= cols_idx) & (rows_idx < cols_idx + LANES)).astype(ml_dtypes.bfloat16)
+    return ((rows_idx >= cols_idx) & (rows_idx < cols_idx + LANES)).astype(ml_dtypes.bfloat16)
+
+
+def slide(fields, groups, local_chan):
     vmem = pl.BlockSpec(memory_space=VMEM)
     return pl.pallas_call(
         slide_kernel,
@@ -331,12 +341,12 @@
         scratch_shapes=[VMEM((local_chan, 64 + 2 * REACH + 8, LANES), jnp.float32)],
         compiler_params=pltpu.CompilerParams(vmem_limit_bytes=24 * 1024 * 1024),
         name="slide",
-    )(fields, table)
-
-
-def cross_kernel(starts_ref, lengths_ref, in_ref, out_ref, gathered, weights, uppers, lowers):
+    )(fields, slide_table())
+
+
+def cross_kernel(starts_ref, lengths_ref, in_ref, out_ref, weights, uppers, lowers):
     channels = starts_ref.shape[0]
-    shifts = weights.shape[2] // LANES
+    shifts = 2 * HALO // LANES
     own = out_ref.shape[1]
     taken = in_ref.shape[0] // channels
     starts, lengths = starts_ref[...], lengths_ref[...]
@@ -345,25 +355,23 @@
         jnp.int32, starts.shape, 1
     )
     nothing = jnp.zeros_like(inverse)
-    weights[...] = jnp.zeros_like(weights)
     for shift in range(shifts):
         offset = LANES * shift - HALO
         inside = (starts <= offset) & (offset + LANES <= starts + lengths)
-        values = halves(jnp.where(inside & others, inverse, nothing))
-        for k in range(2):
-            weights[k, :, shift * LANES : shift * LANES + channels] = values[k]
-    gathered[...] = jnp.zeros_like(gathered)
+        weights[:, shift * channels : (shift + 1) * channels] = jnp.where(
+            inside & others, inverse, nothing
+        )
     for step in range(taken - 1):
-        gathered[:channels, :] = in_ref[pl.ds(step, channels, stride=taken), :]
-        at = slice(step * LANES, (step + 1) * LANES)
-        uppers[at, :], lowers[at, :] = halves(gathered[...])
-    pair_weights = (weights[0], weights[1])
+        at = slice(step * channels, (step + 1) * channels)
+        uppers[at, :], lowers[at, :] = halves(in_ref[pl.ds(step, channels, stride=taken), :])
+    pair_weights = halves(weights[...])
     for step in range(0, own, 2):
 
         def pair(ref):
-            low, depth = step * LANES, shifts * LANES
+            low, depth = step * channels, shifts * channels
             return jnp.concatenate(
-                [ref[low : low + depth, :], ref[low + LANES : low + LANES + depth, :]], axis=1
+                [ref[low : low + depth, :], ref[low + channels : low + channels + depth, :]],
+                axis=1,
             )
 
         both = triple(pair_weights, (pair(uppers), pair(lowers)))
@@ -374,7 +382,7 @@
 def cross(starts, lengths, blocks, own):
     channels = starts.shape[0]
     shifts = 2 * HALO // LANES
-    taken = blocks.shape[2]
+    rows = (blocks.shape[2] - 1) * channels
     vmem = pl.BlockSpec(memory_space=VMEM)
     return pl.pallas_call(
         cross_kernel,
@@ -382,10 +390,9 @@
         out_specs=vmem,
         out_shape=jax.ShapeDtypeStruct((channels, own, LANES), jnp.float32),
         scratch_shapes=[
-            VMEM((LANES, LANES), jnp.float32),
-            VMEM((2, channels, shifts * LANES), jnp.bfloat16),
-            VMEM(((taken - 1) * LANES, LANES), jnp.bfloat16),
-            VMEM(((taken - 1) * LANES, LANES), jnp.bfloat16),
+            VMEM((channels, shifts * channels), jnp.float32),
+            VMEM((rows, LANES), jnp.bfloat16),
+            VMEM((rows, LANES), jnp.bfloat16),
         ],
         name="cross",
     )(starts, lengths, blocks.reshape(-1, LANES))
@@ -414,8 +421,7 @@
     for chan in range(out_ref.shape[1]):
         fields = fields_of(held, chan)
         others = cross_ref[:, chan].reshape(64, LANES)
-        powers = sum(real * real + imag * imag for real, imag in fields)
-        cosine, sine = cosine_and_sine(GAMMA_SELF * powers + GAMMA_CROSS * others)
+        cosine, sine = cosine_and_sine(GAMMA_SELF * total(fields) + GAMMA_CROSS * others)
         for pol, (real, imag) in enumerate(fields):
             at = pl.ds(pol, 64, stride=2)
             out_ref[0, chan, at, :] = cosine * real - sine * imag
@@ -446,14 +452,13 @@
 def per_device(launched, amp_noise, window_start, window_length):
     local_chan = launched.shape[1]
     groups = lax.axis_size("chan")
-    place = lax.axis_index("j").astype(jnp.int32).reshape(1)
     own_tables = lax.dynamic_index_in_dim(
         jnp.asarray(tables()[3]), lax.axis_index("i"), 0, keepdims=False
     )
     values = exchange(head(launched), "j")
     values = exchange(fold(values), "i")
     values = exchange(disperse(values, own_tables), "i")
-    fields = exchange(unfold(values, place), "j")
+    fields = exchange(unfold(values), "j")
     blocks = exchange(slide(fields, groups, local_chan), "chan")
     cross_sum = cross(window_start, window_length, blocks, 64 // groups)
     cross_sum = exchange(cross_sum.reshape(groups, local_chan, -1, LANES), "chan")

time: 278 us -> 274 us (0.986)
  blocking collectives: 207 us -> 232 us
  waiting for transfers between devices: 40.7 us -> 18.6 us
  starting transfers between devices: 7.17 us -> 3.58 us
    all_to_all x4 -> x5, blocking collectives: 207 us -> 232 us  [exchange(): return lax.all_to_all(values, axis, 0, 0, tiled=True)]
    all_to_all x2 -> x1, waiting for transfers between devices: 40.7 us -> 18.6 us  [exchange(): return lax.all_to_all(values, axis, 0, 0, tiled=True)]
    all_to_all x2 -> x1, starting transfers between devices: 7.17 us -> 3.58 us  [exchange(): return lax.all_to_all(values, axis, 0, 0, tiled=True)]
  transfers between devices with their start and end apart: 2 -> 1, of which waited for: 2 -> 1; matrix products, arithmetic and copies ran while one was open for 0% -> 1% of each run, Pallas kernels for 0% -> 0%
where the time goes in v3:
time: 274 us; the launch traced here: 273 us
  blocking collectives  232 us (85%)
  waiting for transfers between devices  18.6 us (7%)
  Pallas kernels  16.8 us (6%)
  starting transfers between devices  3.58 us (1%)
    all_to_all x5, blocking collectives, exchange(): return lax.all_to_all(values, axis, 0, 0, tiled=True)  232 us
    all_to_all x1, waiting for transfers between devices, exchange(): return lax.all_to_all(values, axis, 0, 0, tiled=True)  18.6 us
    pallas_call x1, Pallas kernels, disperse(): pl.pallas_call(disperse_kernel, in_specs=[vmem] * 5, out_specs=vmem, out_...  5.74 us
  transfers between devices with their start and end apart: 1, of which 1 were waited for; matrix products, arithmetic and copies ran while one was open for 1% of the time, Pallas kernels for 0%

profile of v3, /device:TPU:64, one launch (start us, length us, event | category | flops | bytes accessed | tf_op | source)
XLA Modules:
  0.0 273.5 jit_solution(10794491042270140909)
XLA Ops:
  0.0 2.7 head.1
  2.7 90.9 %all_to_all.30.in_ref = f32[8,2,3,64,128]{4,3,2,1,0:T(8,128)} all-to-all(f32[8,2,3,64,128]{4,3,2,1,0:T(8,128)} %head.1), channel_id=1, replica_groups=mesh['chan'=8,'j'=8,'i'=8] {'j'}, dimensions={0} | all-to-all | bytes 3145728 | tf_op jit(solution)/shard_map/all_to_all | solution.py:449
  93.6 2.4 fold.1
  96.0 3.6 %all-to-all-start.1 = ((f32[8,2,3,64,128]{4,3,2,1,0:T(8,128)}), f32[8,2,3,64,128]{4,3,2,1,0:T(8,128)S(1)}, u32[]{:S(2)}, u32[]{:S(2)}) async-start(f32[8,2,3,64,128]{4,3,2,1,0:T(8,128)} %fold.1), calls=%async_computation.1 | async-start | bytes 3145728 | tf_op jit(solution)/shard_map/all_to_all | solution.py:449
  99.6 0.0 copy-start.2
  99.6 0.0 copy-start.3
  99.6 1.4 dynamic-slice_bitcast_fusion.own_ref
  101.0 18.6 %all-to-all-done.1.in_ref = f32[8,2,3,64,128]{4,3,2,1,0:T(8,128)S(1)} async-done(((f32[8,2,3,64,128]{4,3,2,1,0:T(8,128)}), f32[8,2,3,64,128]{4,3,2,1,0:T(8,128)S(1)}, u32[]{:S(2)}, u32[]{:S(2)}) %all-to-all-start.1) | async-done | bytes 1572896 | tf_op jit(solution)/shard_map/all_to_all | solution.py:449
  119.6 0.0 copy-done.2
  119.6 0.0 copy-done.3
  119.6 1.2 copy-done
  120.8 5.7 %disperse.1 = f32[8,2,3,72,128]{4,3,2,1,0:T(8,128)S(1)} custom-call(f32[8,2,3,64,128]{4,3,2,1,0:T(8,128)S(1)} %all-to-all-done.1.in_ref, bf16[4,2,256,256]{3,2,1,0:T(8,128)(2,1)S(1)} %copy-done, f32[2,256,128]{2,1,0:T(8,128)S(1)} %copy-done.3, f32[2,512,128]{2,1,0:T(8,128)S(1)} %copy-done.2, f32[4,520,128]{2,1,0:T(8,128)S(1)} %dynamic-slice_bitcast_fusion.own_ref), custom_call_target="tpu_custom_call" | custom-call | tf_op jit(solution)/shard_map/disperse/pallas_call | solution.py:238
  126.6 25.3 %all_to_all.31.in_ref = f32[8,2,3,72,128]{4,3,2,1,0:T(8,128)S(1)} all-to-all(f32[8,2,3,72,128]{4,3,2,1,0:T(8,128)S(1)} %disperse.1), channel_id=1, replica_groups=mesh['chan'=8,'j'=8,'i'=8] {'i'}, dimensions={0} | all-to-all | bytes 3538944 | tf_op jit(solution)/shard_map/all_to_all | solution.py:449
  151.9 0.3 unfold.1
  152.1 0.0 copy-start.4
  152.2 82.8 %all_to_all.32.held = f32[8,400,128]{2,1,0:T(8,128)S(1)} all-to-all(f32[8,400,128]{2,1,0:T(8,128)S(1)} %unfold.1), channel_id=1, replica_groups=mesh['chan'=8,'j'=8,'i'=8] {'j'}, dimensions={0} | all-to-all | bytes 3276800 | tf_op jit(solution)/shard_map/all_to_all | solution.py:449
  235.0 0.0 copy-done.4
  235.0 0.4 slide.1
  235.4 0.0 copy-start.1
  235.4 20.0 %all_to_all.33 = f32[8,12,16,128]{3,2,1,0:T(8,128)} all-to-all(f32[8,12,16,128]{3,2,1,0:T(8,128)S(1)} %slide.1), channel_id=1, replica_groups=mesh['chan'=8,'j'=8,'i'=8] {'chan'}, dimensions={0} | all-to-all | bytes 1572864 | tf_op jit(solution)/shard_map/all_to_all | solution.py:449
  255.4 3.2 %cross.1 = f32[96,8,128]{2,1,0:T(8,128)} custom-call(s32[96,96]{1,0:T(8,128)} %starts_ref.1, s32[96,96]{1,0:T(8,128)} %lengths_ref.1, f32[1536,128]{1,0:T(8,128)} %bitcast.20), custom_call_target="tpu_custom_call" | custom-call | tf_op jit(solution)/shard_map/cross/pallas_call | solution.py:387
  258.6 12.7 %all_to_all.34.cross_ref = f32[8,12,8,128]{3,2,1,0:T(8,128)S(1)} all-to-all(f32[8,12,8,128]{3,2,1,0:T(8,128)} %bitcast.22), channel_id=1, replica_groups=mesh['chan'=8,'j'=8,'i'=8] {'chan'}, dimensions={0} | all-to-all | bytes 786432 | tf_op jit(solution)/shard_map/all_to_all | solution.py:449
  271.3 0.0 copy-done.1
  271.3 2.1 tail.1
  (1 shorter events, 0.0 us)
Async XLA Ops:
  96.0 23.6 %all-to-all-start.1 = ((f32[8,2,3,64,128]{4,3,2,1,0:T(8,128)}), f32[8,2,3,64,128]{4,3,2,1,0:T(8,128)S(1)}, u32[]{:S(2)}, u32[]{:S(2)}) async-start(f32[8,2,3,64,128]{4,3,2,1,0:T(8,128)} %fold.1), calls=%async_computation.1 | async-start | bytes 3145728 | tf_op jit(solution)/shard_map/all_to_all | solution.py:449
  99.6 20.0 %copy-start.2 = (f32[2,512,128]{2,1,0:T(8,128)S(1)}, f32[2,512,128]{2,1,0:T(8,128)}, u32[]{:S(2)}) copy-start(f32[2,512,128]{2,1,0:T(8,128)} %constant.23.clone.turn_ref) | copy-start | bytes 1572868
  99.6 20.0 %copy-start.3 = (f32[2,256,128]{2,1,0:T(8,128)S(1)}, f32[2,256,128]{2,1,0:T(8,128)}, u32[]{:S(2)}) copy-start(f32[2,256,128]{2,1,0:T(8,128)} %constant.22.clone.middle_ref) | copy-start | bytes 786436
  119.6 1.2 copy-start
  152.1 82.8 %copy-start.4 = (bf16[256,128]{1,0:T(8,128)(2,1)S(1)}, bf16[256,128]{1,0:T(8,128)(2,1)}, u32[]{:S(2)}) copy-start(bf16[256,128]{1,0:T(8,128)(2,1)} %constant.24.clone.table_ref) | copy-start | bytes 196612
  235.4 35.9 %copy-start.1 = (bf16[2,12,2,8192]{3,2,1,0:T(2,128)(2,1)S(1)}, bf16[2,12,2,8192]{3,2,1,0:T(2,128)(2,1)}, u32[]{:S(2)}) copy-start(bf16[2,12,2,8192]{3,2,1,0:T(2,128)(2,1)} %param.10) | copy-start | bytes 2359300

commit v4 on v3

--- a/solution.py
+++ b/solution.py
@@ -20,6 +20,8 @@
 OUTER = FOLDED // LANES
 REACH = HALO // LANES
 WHOLE = 8
+GROUP = 8
+TAKEN = 64 // GROUP + 1
 FIELD_ROWS = 2 * 3 * 64
 SMEM = pltpu.SMEM
 VMEM = pltpu.VMEM
@@ -314,15 +316,42 @@
     return sum(real * real + imag * imag for real, imag in fields)
 
 
-def slide_kernel(held, table_ref, out_ref, extended):
-    groups, local_chan, taken, _ = out_ref.shape
+def trade(arrays):
+    lanes = lax.broadcasted_iota(jnp.int32, arrays[0].shape, 1) // (LANES // GROUP)
+    arrays = list(arrays)
+    for bit in (1, 2, 4):
+        width = bit * (LANES // GROUP)
+        upper_half = (lanes & bit) != 0
+        for low in range(GROUP):
+            if low & bit:
+                continue
+            first, second = arrays[low], arrays[low | bit]
+            arrays[low] = jnp.where(upper_half, pltpu.roll(second, width, 1), first)
+            arrays[low | bit] = jnp.where(
+                upper_half, second, pltpu.roll(first, LANES - width, 1)
+            )
+    return arrays
+
+
+def slide_kernel(held, table_ref, out_ref, extended, sliding):
+    local_chan = extended.shape[0]
+    span = 64 + 2 * REACH
+    rows = local_chan * TAKEN
     table = table_ref[...]
     for chan in range(local_chan):
         powers = total(fields_of(held, chan))
         around = powers_around(held, chan)
-        sliding = sliding_sums(powers, around, table, extended.at[chan])
-        for group in range(groups):
-            out_ref[group, chan] = sliding[8 * group : 8 * group + taken]
+        sliding[span * chan : span * chan + span, :] = sliding_sums(
+            powers, around, table, extended.at[chan]
+        )
+    for low in range(0, rows, 32):
+        count = min(32, rows - low)
+        parts = [
+            sliding[pl.ds(low * GROUP + k, count, stride=GROUP), :] for k in range(GROUP)
+        ]
+        for group, part in enumerate(trade(parts)):
+            out_ref[group, low : low + count, :] = part
+    out_ref[:, rows:, :] = jnp.zeros_like(out_ref[:, rows:, :])
 
 
 def slide_table():
@@ -337,18 +366,24 @@
         slide_kernel,
         in_specs=[vmem, vmem],
         out_specs=vmem,
-        out_shape=jax.ShapeDtypeStruct((groups, local_chan, 16, LANES), jnp.float32),
-        scratch_shapes=[VMEM((local_chan, 64 + 2 * REACH + 8, LANES), jnp.float32)],
+        out_shape=jax.ShapeDtypeStruct(
+            (groups, -(-local_chan * TAKEN // 8) * 8, LANES), jnp.float32
+        ),
+        scratch_shapes=[
+            VMEM((local_chan, 64 + 2 * REACH + 8, LANES), jnp.float32),
+            VMEM((local_chan * (64 + 2 * REACH), LANES), jnp.float32),
+        ],
         compiler_params=pltpu.CompilerParams(vmem_limit_bytes=24 * 1024 * 1024),
         name="slide",
     )(fields, slide_table())
 
 
-def cross_kernel(starts_ref, lengths_ref, in_ref, out_ref, weights, uppers, lowers):
+def cross_kernel(starts_ref, lengths_ref, in_ref, out_ref, gathered, weights, uppers, lowers):
     channels = starts_ref.shape[0]
+    devices = in_ref.shape[0]
+    each = channels // devices
     shifts = 2 * HALO // LANES
-    own = out_ref.shape[1]
-    taken = in_ref.shape[0] // channels
+    width = LANES // GROUP
     starts, lengths = starts_ref[...], lengths_ref[...]
     inverse = 1.0 / lengths.astype(jnp.float32)
     others = lax.broadcasted_iota(jnp.int32, starts.shape, 0) != lax.broadcasted_iota(
@@ -361,41 +396,52 @@
         weights[:, shift * channels : (shift + 1) * channels] = jnp.where(
             inside & others, inverse, nothing
         )
-    for step in range(taken - 1):
-        at = slice(step * channels, (step + 1) * channels)
-        uppers[at, :], lowers[at, :] = halves(in_ref[pl.ds(step, channels, stride=taken), :])
+    for step in range(TAKEN):
+        for device in range(devices):
+            gathered[step, device * each : (device + 1) * each, :] = in_ref[
+                device, pl.ds(step, each, stride=TAKEN), :
+            ]
+    lanes = lax.broadcasted_iota(jnp.int32, (channels, LANES), 1)
+    for shift in range(shifts):
+        moved = [
+            pltpu.roll(gathered[step], LANES - width * shift, 1) if shift else gathered[step]
+            for step in range(TAKEN)
+        ]
+        at = slice(shift * channels, (shift + 1) * channels)
+        for step in range(TAKEN - 1):
+            values = moved[step]
+            if shift:
+                values = jnp.where(lanes < LANES - width * shift, values, moved[step + 1])
+            uppers[step, at, :], lowers[step, at, :] = halves(values)
     pair_weights = halves(weights[...])
-    for step in range(0, own, 2):
+    for step in range(0, TAKEN - 1, 2):
 
         def pair(ref):
-            low, depth = step * channels, shifts * channels
-            return jnp.concatenate(
-                [ref[low : low + depth, :], ref[low + channels : low + channels + depth, :]],
-                axis=1,
-            )
+            return jnp.concatenate([ref[step], ref[step + 1]], axis=1)
 
         both = triple(pair_weights, (pair(uppers), pair(lowers)))
         out_ref[:, step, :] = both[:, :LANES]
         out_ref[:, step + 1, :] = both[:, LANES:]
 
 
-def cross(starts, lengths, blocks, own):
+def cross(starts, lengths, blocks):
     channels = starts.shape[0]
-    shifts = 2 * HALO // LANES
-    rows = (blocks.shape[2] - 1) * channels
+    depth = 2 * HALO // LANES * channels
     vmem = pl.BlockSpec(memory_space=VMEM)
     return pl.pallas_call(
         cross_kernel,
         in_specs=[vmem] * 3,
         out_specs=vmem,
-        out_shape=jax.ShapeDtypeStruct((channels, own, LANES), jnp.float32),
+        out_shape=jax.ShapeDtypeStruct((channels, TAKEN - 1, LANES), jnp.float32),
         scratch_shapes=[
-            VMEM((channels, shifts * channels), jnp.float32),
-            VMEM((rows, LANES), jnp.bfloat16),
-            VMEM((rows, LANES), jnp.bfloat16),
+            VMEM((TAKEN, channels, LANES), jnp.float32),
+            VMEM((channels, depth), jnp.float32),
+            VMEM((TAKEN - 1, depth, LANES), jnp.bfloat16),
+            VMEM((TAKEN - 1, depth, LANES), jnp.bfloat16),
         ],
+        compiler_params=pltpu.CompilerParams(vmem_limit_bytes=24 * 1024 * 1024),
         name="cross",
-    )(starts, lengths, blocks.reshape(-1, LANES))
+    )(starts, lengths, blocks)
 
 
 def cosine_and_sine(angles):
@@ -417,10 +463,15 @@
     return jnp.where(turned, -near, near), jnp.where(quadrant >= 2, -far, far)
 
 
-def tail_kernel(held, cross_ref, noise_ref, out_ref):
+def tail_kernel(held, cross_ref, noise_ref, out_ref, cross_sum):
+    rows = cross_ref.shape[1]
+    for low in range(0, rows, 32):
+        parts = [cross_ref[group, low : low + 32, :] for group in range(GROUP)]
+        for k, part in enumerate(trade(parts)):
+            cross_sum[pl.ds(low * GROUP + k, 32, stride=GROUP), :] = part
     for chan in range(out_ref.shape[1]):
         fields = fields_of(held, chan)
-        others = cross_ref[:, chan].reshape(64, LANES)
+        others = cross_sum[64 * chan : 64 * chan + 64, :]
         cosine, sine = cosine_and_sine(GAMMA_SELF * total(fields) + GAMMA_CROSS * others)
         for pol, (real, imag) in enumerate(fields):
             at = pl.ds(pol, 64, stride=2)
@@ -431,13 +482,14 @@
 
 
 def tail(fields, cross_sum, amp_noise):
-    local_chan = cross_sum.shape[1]
+    local_chan = cross_sum.shape[1] * GROUP // 64
     vmem = pl.BlockSpec(memory_space=VMEM)
     received = pl.pallas_call(
         tail_kernel,
         in_specs=[vmem] * 3,
         out_specs=vmem,
         out_shape=jax.ShapeDtypeStruct((2, local_chan, 128, LANES), jnp.float32),
+        scratch_shapes=[VMEM((64 * local_chan, LANES), jnp.float32)],
         compiler_params=pltpu.CompilerParams(vmem_limit_bytes=24 * 1024 * 1024),
         name="tail",
     )(fields, cross_sum, interleaved(amp_noise))
@@ -460,8 +512,8 @@
     values = exchange(disperse(values, own_tables), "i")
     fields = exchange(unfold(values), "j")
     blocks = exchange(slide(fields, groups, local_chan), "chan")
-    cross_sum = cross(window_start, window_length, blocks, 64 // groups)
-    cross_sum = exchange(cross_sum.reshape(groups, local_chan, -1, LANES), "chan")
+    cross_sum = cross(window_start, window_length, blocks)
+    cross_sum = exchange(cross_sum.reshape(groups, -1, LANES), "chan")
     return tail(fields, cross_sum, amp_noise)
 
 

time: 274 us -> 270 us (0.985)
  the two profiles are of different devices: /device:TPU:64 before, /device:TPU:2 now
where the time goes in v4:
time: 270 us
  blocking collectives  227 us (84%)
  waiting for transfers between devices  18.7 us (7%)
  Pallas kernels  16.1 us (6%)
  starting transfers between devices  4.83 us (2%)
    all_to_all x5, blocking collectives, exchange(): return lax.all_to_all(values, axis, 0, 0, tiled=True)  227 us
    all_to_all x1, waiting for transfers between devices, exchange(): return lax.all_to_all(values, axis, 0, 0, tiled=True)  18.7 us
    pallas_call x1, Pallas kernels, disperse(): pl.pallas_call(disperse_kernel, in_specs=[vmem] * 5, out_specs=vmem, out_...  5.74 us
  transfers between devices with their start and end apart: 1, of which 1 were waited for; matrix products, arithmetic and copies ran while one was open for 1% of the time, Pallas kernels for 0%

profile of v4, /device:TPU:2, one launch (start us, length us, event | category | flops | bytes accessed | tf_op | source)
XLA Modules:
  0.0 269.8 jit_solution(17975010924052404440)
XLA Ops:
  0.0 2.7 head.1
  2.7 87.3 %all_to_all.30.in_ref = f32[8,2,3,64,128]{4,3,2,1,0:T(8,128)} all-to-all(f32[8,2,3,64,128]{4,3,2,1,0:T(8,128)} %head.1), channel_id=1, replica_groups=mesh['chan'=8,'j'=8,'i'=8] {'j'}, dimensions={0} | all-to-all | bytes 3145728 | tf_op jit(solution)/shard_map/all_to_all | solution.py:501
  89.9 2.4 fold.1
  92.4 4.8 %all-to-all-start.1 = ((f32[8,2,3,64,128]{4,3,2,1,0:T(8,128)}), f32[8,2,3,64,128]{4,3,2,1,0:T(8,128)S(1)}, u32[]{:S(2)}, u32[]{:S(2)}) async-start(f32[8,2,3,64,128]{4,3,2,1,0:T(8,128)} %fold.1), calls=%async_computation.1 | async-start | bytes 3145728 | tf_op jit(solution)/shard_map/all_to_all | solution.py:501
  97.2 0.0 copy-start.3
  97.2 1.4 dynamic-slice_bitcast_fusion.own_ref
  98.6 18.7 %all-to-all-done.1.in_ref = f32[8,2,3,64,128]{4,3,2,1,0:T(8,128)S(1)} async-done(((f32[8,2,3,64,128]{4,3,2,1,0:T(8,128)}), f32[8,2,3,64,128]{4,3,2,1,0:T(8,128)S(1)}, u32[]{:S(2)}, u32[]{:S(2)}) %all-to-all-start.1) | async-done | bytes 1572896 | tf_op jit(solution)/shard_map/all_to_all | solution.py:501
  117.3 0.0 copy-done.2
  117.3 0.0 copy-done.3
  117.3 1.2 copy-done
  118.5 5.7 %disperse.1 = f32[8,2,3,72,128]{4,3,2,1,0:T(8,128)S(1)} custom-call(f32[8,2,3,64,128]{4,3,2,1,0:T(8,128)S(1)} %all-to-all-done.1.in_ref, bf16[4,2,256,256]{3,2,1,0:T(8,128)(2,1)S(1)} %copy-done, f32[2,256,128]{2,1,0:T(8,128)S(1)} %copy-done.3, f32[2,512,128]{2,1,0:T(8,128)S(1)} %copy-done.2, f32[4,520,128]{2,1,0:T(8,128)S(1)} %dynamic-slice_bitcast_fusion.own_ref), custom_call_target="tpu_custom_call" | custom-call | tf_op jit(solution)/shard_map/disperse/pallas_call | solution.py:240
  124.2 25.3 %all_to_all.31.in_ref = f32[8,2,3,72,128]{4,3,2,1,0:T(8,128)S(1)} all-to-all(f32[8,2,3,72,128]{4,3,2,1,0:T(8,128)S(1)} %disperse.1), channel_id=1, replica_groups=mesh['chan'=8,'j'=8,'i'=8] {'i'}, dimensions={0} | all-to-all | bytes 3538944 | tf_op jit(solution)/shard_map/all_to_all | solution.py:501
  149.6 0.3 unfold.1
  149.8 0.0 copy-start.4
  149.8 87.3 %all_to_all.32.held = f32[8,400,128]{2,1,0:T(8,128)S(1)} all-to-all(f32[8,400,128]{2,1,0:T(8,128)S(1)} %unfold.1), channel_id=1, replica_groups=mesh['chan'=8,'j'=8,'i'=8] {'j'}, dimensions={0} | all-to-all | bytes 3276800 | tf_op jit(solution)/shard_map/all_to_all | solution.py:501
  237.1 0.0 copy-done.4
  237.1 0.7 slide.1
  237.8 0.0 copy-start.1
  237.9 15.3 %all_to_all.33.in_ref = f32[8,112,128]{2,1,0:T(8,128)S(1)} all-to-all(f32[8,112,128]{2,1,0:T(8,128)S(1)} %slide.1), channel_id=1, replica_groups=mesh['chan'=8,'j'=8,'i'=8] {'chan'}, dimensions={0} | all-to-all | bytes 917504 | tf_op jit(solution)/shard_map/all_to_all | solution.py:501
  253.1 0.0 copy-done.5
  253.1 0.0 copy-done.6
  253.1 1.8 cross.1
  255.0 12.3 %all_to_all.34.cross_ref = f32[8,96,128]{2,1,0:T(8,128)S(1)} all-to-all(f32[8,96,128]{2,1,0:T(8,128)S(1)} %bitcast.18), channel_id=1, replica_groups=mesh['chan'=8,'j'=8,'i'=8] {'chan'}, dimensions={0} | all-to-all | bytes 786432 | tf_op jit(solution)/shard_map/all_to_all | solution.py:501
  267.3 2.6 tail.1
  (5 shorter events, 0.0 us)
Async XLA Ops:
  92.4 24.9 %all-to-all-start.1 = ((f32[8,2,3,64,128]{4,3,2,1,0:T(8,128)}), f32[8,2,3,64,128]{4,3,2,1,0:T(8,128)S(1)}, u32[]{:S(2)}, u32[]{:S(2)}) async-start(f32[8,2,3,64,128]{4,3,2,1,0:T(8,128)} %fold.1), calls=%async_computation.1 | async-start | bytes 3145728 | tf_op jit(solution)/shard_map/all_to_all | solution.py:501
  97.2 20.1 %copy-start.2 = (f32[2,512,128]{2,1,0:T(8,128)S(1)}, f32[2,512,128]{2,1,0:T(8,128)}, u32[]{:S(2)}) copy-start(f32[2,512,128]{2,1,0:T(8,128)} %constant.23.clone.turn_ref) | copy-start | bytes 1572868
  97.2 20.1 %copy-start.3 = (f32[2,256,128]{2,1,0:T(8,128)S(1)}, f32[2,256,128]{2,1,0:T(8,128)}, u32[]{:S(2)}) copy-start(f32[2,256,128]{2,1,0:T(8,128)} %constant.22.clone.middle_ref) | copy-start | bytes 786436
  117.3 1.2 copy-start
  149.8 87.3 %copy-start.4 = (bf16[256,128]{1,0:T(8,128)(2,1)S(1)}, bf16[256,128]{1,0:T(8,128)(2,1)}, u32[]{:S(2)}) copy-start(bf16[256,128]{1,0:T(8,128)(2,1)} %constant.24.clone.table_ref) | copy-start | bytes 196612
  237.1 16.0 %copy-start.5 = (s32[96,96]{1,0:T(8,128)S(1)}, s32[96,96]{1,0:T(8,128)}, u32[]{:S(2)}) copy-start(s32[96,96]{1,0:T(8,128)} %starts_ref.1) | copy-start | bytes 110596
  237.1 16.0 %copy-start.6 = (s32[96,96]{1,0:T(8,128)S(1)}, s32[96,96]{1,0:T(8,128)}, u32[]{:S(2)}) copy-start(s32[96,96]{1,0:T(8,128)} %lengths_ref.1) | copy-start | bytes 110596
  237.8 29.4 %copy-start.1 = (bf16[2,12,2,8192]{3,2,1,0:T(2,128)(2,1)S(1)}, bf16[2,12,2,8192]{3,2,1,0:T(2,128)(2,1)}, u32[]{:S(2)}) copy-start(bf16[2,12,2,8192]{3,2,1,0:T(2,128)(2,1)} %param.10) | copy-start | bytes 2359300

commit v5 on v4

--- a/solution.py
+++ b/solution.py
@@ -122,6 +122,7 @@
         in_specs=[vmem],
         out_specs=vmem,
         out_shape=jax.ShapeDtypeStruct((COARSE, 2, 3, 64, LANES), jnp.float32),
+        compiler_params=pltpu.CompilerParams(vmem_limit_bytes=24 * 1024 * 1024),
         name="head",
     )(interleaved(launched))
 
@@ -145,13 +146,13 @@
 
 
 def fold(values):
-    spec = pl.BlockSpec((COARSE, 2, 3, 32, LANES), lambda k: (0, 0, 0, k, 0))
+    vmem = pl.BlockSpec(memory_space=VMEM)
     return pl.pallas_call(
         fold_kernel,
-        grid=(2,),
-        in_specs=[spec],
-        out_specs=spec,
+        in_specs=[vmem],
+        out_specs=vmem,
         out_shape=jax.ShapeDtypeStruct(values.shape, jnp.float32),
+        compiler_params=pltpu.CompilerParams(vmem_limit_bytes=24 * 1024 * 1024),
         name="fold",
     )(values)
 
@@ -463,22 +464,32 @@
     return jnp.where(turned, -near, near), jnp.where(quadrant >= 2, -far, far)
 
 
-def tail_kernel(held, cross_ref, noise_ref, out_ref, cross_sum):
+def tail_kernel(held, cross_ref, noise_ref, out_ref, cross_sum, found, sent):
     rows = cross_ref.shape[1]
     for low in range(0, rows, 32):
         parts = [cross_ref[group, low : low + 32, :] for group in range(GROUP)]
         for k, part in enumerate(trade(parts)):
             cross_sum[pl.ds(low * GROUP + k, 32, stride=GROUP), :] = part
+    part = 3
+
+    def send(k):
+        at = (slice(None), pl.ds(k * part, part))
+        return pltpu.make_async_copy(found.at[at], out_ref.at[at], sent.at[k])
+
     for chan in range(out_ref.shape[1]):
         fields = fields_of(held, chan)
         others = cross_sum[64 * chan : 64 * chan + 64, :]
         cosine, sine = cosine_and_sine(GAMMA_SELF * total(fields) + GAMMA_CROSS * others)
         for pol, (real, imag) in enumerate(fields):
             at = pl.ds(pol, 64, stride=2)
-            out_ref[0, chan, at, :] = cosine * real - sine * imag
-            out_ref[1, chan, at, :] = cosine * imag + sine * real
-        for part in range(2):
-            out_ref[part, chan] = out_ref[part, chan] + noise_ref[part, chan].astype(jnp.float32)
+            found[0, chan, at, :] = cosine * real - sine * imag
+            found[1, chan, at, :] = cosine * imag + sine * real
+        for side in range(2):
+            found[side, chan] = found[side, chan] + noise_ref[side, chan].astype(jnp.float32)
+        if chan % part == part - 1:
+            send(chan // part).start()
+    for k in range(out_ref.shape[1] // part):
+        send(k).wait()
 
 
 def tail(fields, cross_sum, amp_noise):
@@ -487,9 +498,13 @@
     received = pl.pallas_call(
         tail_kernel,
         in_specs=[vmem] * 3,
-        out_specs=vmem,
+        out_specs=pl.BlockSpec(memory_space=pl.ANY),
         out_shape=jax.ShapeDtypeStruct((2, local_chan, 128, LANES), jnp.float32),
-        scratch_shapes=[VMEM((64 * local_chan, LANES), jnp.float32)],
+        scratch_shapes=[
+            VMEM((64 * local_chan, LANES), jnp.float32),
+            VMEM((2, local_chan, 128, LANES), jnp.float32),
+            pltpu.SemaphoreType.DMA((local_chan // 3,)),
+        ],
         compiler_params=pltpu.CompilerParams(vmem_limit_bytes=24 * 1024 * 1024),
         name="tail",
     )(fields, cross_sum, interleaved(amp_noise))
@@ -507,8 +522,8 @@
     own_tables = lax.dynamic_index_in_dim(
         jnp.asarray(tables()[3]), lax.axis_index("i"), 0, keepdims=False
     )
-    values = exchange(head(launched), "j")
-    values = exchange(fold(values), "i")
+    values, own_tables = lax.optimization_barrier((head(launched), own_tables))
+    values = exchange(fold(exchange(values, "j")), "i")
     values = exchange(disperse(values, own_tables), "i")
     fields = exchange(unfold(values), "j")
     blocks = exchange(slide(fields, groups, local_chan), "chan")

time: 270 us -> 266 us (0.985)
  blocking collectives: 227 us -> 252 us
  waiting for transfers between devices: 18.7 us -> 0 us
  Pallas kernels: 16.1 us -> 11.2 us
  starting transfers between devices: 4.83 us -> 0 us
    all_to_all x5 -> x6, blocking collectives: 227 us -> 252 us  [exchange(): return lax.all_to_all(values, axis, 0, 0, tiled=True)]
    all_to_all x1 -> x0, waiting for transfers between devices: 18.7 us -> none  [exchange(): return lax.all_to_all(values, axis, 0, 0, tiled=True)]
    all_to_all x1 -> x0, starting transfers between devices: 4.83 us -> none  [exchange(): return lax.all_to_all(values, axis, 0, 0, tiled=True)]
  transfers between devices with their start and end apart: 1 -> 0, of which waited for: 1 -> 0; matrix products, arithmetic and copies ran while one was open for 1% -> 0% of each run, Pallas kernels for 0% -> 0%
where the time goes in v5:
time: 266 us
  blocking collectives  252 us (95%)
  Pallas kernels  11.2 us (4%)
  local copies, waits for them, and re-layouts  2.76 us (1%)
    all_to_all x6, blocking collectives, exchange(): return lax.all_to_all(values, axis, 0, 0, tiled=True)  252 us
    pallas_call x1, Pallas kernels, disperse(): pl.pallas_call(disperse_kernel, in_specs=[vmem] * 5, out_specs=vmem, out_...  5.74 us

profile of v5, /device:TPU:2, one launch (start us, length us, event | category | flops | bytes accessed | tf_op | source)
XLA Modules:
  0.0 265.8 jit_solution(4042392519651630251)
XLA Ops:
  0.0 1.4 copy-done
  1.4 0.1 head.1
  1.5 1.3 dynamic-slice_bitcast_fusion.own_ref
  2.8 87.0 %all_to_all.30.in_ref = f32[8,2,3,64,128]{4,3,2,1,0:T(8,128)S(1)} all-to-all(f32[8,2,3,64,128]{4,3,2,1,0:T(8,128)S(1)} %head.1), channel_id=1, replica_groups=mesh['chan'=8,'j'=8,'i'=8] {'j'}, dimensions={0} | all-to-all | bytes 3145728 | tf_op jit(solution)/shard_map/all_to_all | solution.py:516
  89.8 0.3 fold.1
  90.1 0.0 copy-start.1
  90.1 0.0 copy-start.3
  90.1 0.0 copy-start.4
  90.1 25.1 %all_to_all.31.in_ref = f32[8,2,3,64,128]{4,3,2,1,0:T(8,128)S(1)} all-to-all(f32[8,2,3,64,128]{4,3,2,1,0:T(8,128)S(1)} %fold.1), channel_id=1, replica_groups=mesh['chan'=8,'j'=8,'i'=8] {'i'}, dimensions={0} | all-to-all | bytes 3145728 | tf_op jit(solution)/shard_map/all_to_all | solution.py:516
  115.2 0.0 copy-done.1
  115.2 0.0 copy-done.3
  115.2 5.7 %disperse.1 = f32[8,2,3,72,128]{4,3,2,1,0:T(8,128)S(1)} custom-call(f32[8,2,3,64,128]{4,3,2,1,0:T(8,128)S(1)} %all_to_all.31.in_ref, bf16[4,2,256,256]{3,2,1,0:T(8,128)(2,1)S(1)} %copy-done.1, f32[2,256,128]{2,1,0:T(8,128)S(1)} %copy-done.4, f32[2,512,128]{2,1,0:T(8,128)S(1)} %copy-done.3, f32[4,520,128]{2,1,0:T(8,128)S(1)} %dynamic-slice_bitcast_fusion.own_ref), custom_call_target="tpu_custom_call" | custom-call | tf_op jit(solution)/shard_map/disperse/pallas_call | solution.py:241
  120.9 25.3 %all_to_all.32.in_ref = f32[8,2,3,72,128]{4,3,2,1,0:T(8,128)S(1)} all-to-all(f32[8,2,3,72,128]{4,3,2,1,0:T(8,128)S(1)} %disperse.1), channel_id=1, replica_groups=mesh['chan'=8,'j'=8,'i'=8] {'i'}, dimensions={0} | all-to-all | bytes 3538944 | tf_op jit(solution)/shard_map/all_to_all | solution.py:516
  146.3 0.3 unfold.1
  146.5 0.0 copy-start.5
  146.6 87.1 %all_to_all.33.held = f32[8,400,128]{2,1,0:T(8,128)S(1)} all-to-all(f32[8,400,128]{2,1,0:T(8,128)S(1)} %unfold.1), channel_id=1, replica_groups=mesh['chan'=8,'j'=8,'i'=8] {'j'}, dimensions={0} | all-to-all | bytes 3276800 | tf_op jit(solution)/shard_map/all_to_all | solution.py:516
  233.6 0.7 slide.1
  234.3 0.0 copy-start.2
  234.4 15.0 %all_to_all.34.in_ref = f32[8,112,128]{2,1,0:T(8,128)S(1)} all-to-all(f32[8,112,128]{2,1,0:T(8,128)S(1)} %slide.1), channel_id=1, replica_groups=mesh['chan'=8,'j'=8,'i'=8] {'chan'}, dimensions={0} | all-to-all | bytes 917504 | tf_op jit(solution)/shard_map/all_to_all | solution.py:516
  249.3 0.0 copy-done.6
  249.3 1.8 cross.1
  251.2 12.3 %all_to_all.35.cross_ref = f32[8,96,128]{2,1,0:T(8,128)S(1)} all-to-all(f32[8,96,128]{2,1,0:T(8,128)S(1)} %bitcast.19), channel_id=1, replica_groups=mesh['chan'=8,'j'=8,'i'=8] {'chan'}, dimensions={0} | all-to-all | bytes 786432 | tf_op jit(solution)/shard_map/all_to_all | solution.py:516
  263.5 0.0 copy-done.2
  263.5 2.3 tail.1
  (6 shorter events, 0.0 us)
Async XLA Ops:
  0.0 1.4 copy-start
  90.1 25.1 %copy-start.1 = (bf16[4,2,256,256]{3,2,1,0:T(8,128)(2,1)S(1)}, bf16[4,2,256,256]{3,2,1,0:T(8,128)(2,1)}, u32[]{:S(2)}) copy-start(bf16[4,2,256,256]{3,2,1,0:T(8,128)(2,1)} %constant.21.clone.dft_ref) | copy-start | bytes 3145732
  90.1 25.1 %copy-start.3 = (f32[2,512,128]{2,1,0:T(8,128)S(1)}, f32[2,512,128]{2,1,0:T(8,128)}, u32[]{:S(2)}) copy-start(f32[2,512,128]{2,1,0:T(8,128)} %constant.23.clone.turn_ref) | copy-start | bytes 1572868
  90.1 25.1 %copy-start.4 = (f32[2,256,128]{2,1,0:T(8,128)S(1)}, f32[2,256,128]{2,1,0:T(8,128)}, u32[]{:S(2)}) copy-start(f32[2,256,128]{2,1,0:T(8,128)} %constant.22.clone.middle_ref) | copy-start | bytes 786436
  146.5 87.1 %copy-start.5 = (bf16[256,128]{1,0:T(8,128)(2,1)S(1)}, bf16[256,128]{1,0:T(8,128)(2,1)}, u32[]{:S(2)}) copy-start(bf16[256,128]{1,0:T(8,128)(2,1)} %constant.24.clone.table_ref) | copy-start | bytes 196612
  233.6 15.7 %copy-start.6 = (s32[96,96]{1,0:T(8,128)S(1)}, s32[96,96]{1,0:T(8,128)}, u32[]{:S(2)}) copy-start(s32[96,96]{1,0:T(8,128)} %starts_ref.1) | copy-start | bytes 110596
  233.6 15.7 %copy-start.7 = (s32[96,96]{1,0:T(8,128)S(1)}, s32[96,96]{1,0:T(8,128)}, u32[]{:S(2)}) copy-start(s32[96,96]{1,0:T(8,128)} %lengths_ref.1) | copy-start | bytes 110596
  234.3 29.1 %copy-start.2 = (bf16[2,12,2,8192]{3,2,1,0:T(2,128)(2,1)S(1)}, bf16[2,12,2,8192]{3,2,1,0:T(2,128)(2,1)}, u32[]{:S(2)}) copy-start(bf16[2,12,2,8192]{3,2,1,0:T(2,128)(2,1)} %param.10) | copy-start | bytes 2359300

commit v6 on v5

--- a/solution.py
+++ b/solution.py
@@ -108,23 +108,23 @@
     return ((group, 0), (group, 1), (WHOLE + group // 2, group % 2))
 
 
-def head_kernel(in_ref, out_ref):
+def head_kernel(in_ref, tables_ref, out_ref):
     for group in range(COARSE):
         for row, (chan, pol) in enumerate(rows_of(group)):
             for part in range(2):
                 out_ref[group, part, row] = in_ref[part, chan, pl.ds(pol, 64, stride=2), :]
 
 
-def head(launched):
+def head(launched, own_tables):
     vmem = pl.BlockSpec(memory_space=VMEM)
     return pl.pallas_call(
         head_kernel,
-        in_specs=[vmem],
+        in_specs=[vmem, vmem],
         out_specs=vmem,
         out_shape=jax.ShapeDtypeStruct((COARSE, 2, 3, 64, LANES), jnp.float32),
         compiler_params=pltpu.CompilerParams(vmem_limit_bytes=24 * 1024 * 1024),
         name="head",
-    )(interleaved(launched))
+    )(interleaved(launched), own_tables)
 
 
 def interleaved(values):
@@ -522,8 +522,8 @@
     own_tables = lax.dynamic_index_in_dim(
         jnp.asarray(tables()[3]), lax.axis_index("i"), 0, keepdims=False
     )
-    values, own_tables = lax.optimization_barrier((head(launched), own_tables))
-    values = exchange(fold(exchange(values, "j")), "i")
+    values = exchange(head(launched, own_tables), "j")
+    values = exchange(fold(values), "i")
     values = exchange(disperse(values, own_tables), "i")
     fields = exchange(unfold(values), "j")
     blocks = exchange(slide(fields, groups, local_chan), "chan")

time: 266 us -> 265 us (level)
  no operation moved by 1% of the time
where the time goes in v6:
time: 265 us
  blocking collectives  252 us (95%)
  Pallas kernels  11.2 us (4%)
    all_to_all x6, blocking collectives, exchange(): return lax.all_to_all(values, axis, 0, 0, tiled=True)  252 us
    pallas_call x1, Pallas kernels, disperse(): pl.pallas_call(disperse_kernel, in_specs=[vmem] * 5, out_specs=vmem, out_...  5.74 us

profile of v6, /device:TPU:2, one launch (start us, length us, event | category | flops | bytes accessed | tf_op | source)
XLA Modules:
  0.0 264.8 jit_solution(1118774771475241258)
XLA Ops:
  0.0 1.4 dynamic-slice_bitcast_fusion.tables_ref.own_ref
  1.4 0.3 copy-done
  1.7 0.1 head.1
  1.8 87.0 %all_to_all.30.in_ref = f32[8,2,3,64,128]{4,3,2,1,0:T(8,128)S(1)} all-to-all(f32[8,2,3,64,128]{4,3,2,1,0:T(8,128)S(1)} %head.1), channel_id=1, replica_groups=mesh['chan'=8,'j'=8,'i'=8] {'j'}, dimensions={0} | all-to-all | bytes 3145728 | tf_op jit(solution)/shard_map/all_to_all | solution.py:516
  88.8 0.3 fold.1
  89.1 0.0 copy-start.1
  89.1 0.0 copy-start.3
  89.1 0.0 copy-start.4
  89.1 25.1 %all_to_all.31.in_ref = f32[8,2,3,64,128]{4,3,2,1,0:T(8,128)S(1)} all-to-all(f32[8,2,3,64,128]{4,3,2,1,0:T(8,128)S(1)} %fold.1), channel_id=1, replica_groups=mesh['chan'=8,'j'=8,'i'=8] {'i'}, dimensions={0} | all-to-all | bytes 3145728 | tf_op jit(solution)/shard_map/all_to_all | solution.py:516
  114.2 0.0 copy-done.1
  114.2 0.0 copy-done.3
  114.2 0.0 copy-done.4
  114.2 5.7 %disperse.1 = f32[8,2,3,72,128]{4,3,2,1,0:T(8,128)S(1)} custom-call(f32[8,2,3,64,128]{4,3,2,1,0:T(8,128)S(1)} %all_to_all.31.in_ref, bf16[4,2,256,256]{3,2,1,0:T(8,128)(2,1)S(1)} %copy-done.1, f32[2,256,128]{2,1,0:T(8,128)S(1)} %copy-done.4, f32[2,512,128]{2,1,0:T(8,128)S(1)} %copy-done.3, f32[4,520,128]{2,1,0:T(8,128)S(1)} %dynamic-slice_bitcast_fusion.tables_ref.own_ref), custom_call_target="tpu_custom_call" | custom-call | tf_op jit(solution)/shard_map/disperse/pallas_call | solution.py:241
  119.9 25.3 %all_to_all.32.in_ref = f32[8,2,3,72,128]{4,3,2,1,0:T(8,128)S(1)} all-to-all(f32[8,2,3,72,128]{4,3,2,1,0:T(8,128)S(1)} %disperse.1), channel_id=1, replica_groups=mesh['chan'=8,'j'=8,'i'=8] {'i'}, dimensions={0} | all-to-all | bytes 3538944 | tf_op jit(solution)/shard_map/all_to_all | solution.py:516
  145.3 0.3 unfold.1
  145.5 0.0 copy-start.5
  145.6 87.1 %all_to_all.33.held = f32[8,400,128]{2,1,0:T(8,128)S(1)} all-to-all(f32[8,400,128]{2,1,0:T(8,128)S(1)} %unfold.1), channel_id=1, replica_groups=mesh['chan'=8,'j'=8,'i'=8] {'j'}, dimensions={0} | all-to-all | bytes 3276800 | tf_op jit(solution)/shard_map/all_to_all | solution.py:516
  232.6 0.7 slide.1
  233.3 0.0 copy-start.2
  233.4 15.0 %all_to_all.34.in_ref = f32[8,112,128]{2,1,0:T(8,128)S(1)} all-to-all(f32[8,112,128]{2,1,0:T(8,128)S(1)} %slide.1), channel_id=1, replica_groups=mesh['chan'=8,'j'=8,'i'=8] {'chan'}, dimensions={0} | all-to-all | bytes 917504 | tf_op jit(solution)/shard_map/all_to_all | solution.py:516
  248.3 1.8 cross.1
  250.2 12.3 %all_to_all.35.cross_ref = f32[8,96,128]{2,1,0:T(8,128)S(1)} all-to-all(f32[8,96,128]{2,1,0:T(8,128)S(1)} %bitcast.18), channel_id=1, replica_groups=mesh['chan'=8,'j'=8,'i'=8] {'chan'}, dimensions={0} | all-to-all | bytes 786432 | tf_op jit(solution)/shard_map/all_to_all | solution.py:516
  262.5 0.0 copy-done.2
  262.5 2.3 tail.1
  (6 shorter events, 0.0 us)
Async XLA Ops:
  0.0 1.7 copy-start
  89.1 25.1 %copy-start.1 = (bf16[4,2,256,256]{3,2,1,0:T(8,128)(2,1)S(1)}, bf16[4,2,256,256]{3,2,1,0:T(8,128)(2,1)}, u32[]{:S(2)}) copy-start(bf16[4,2,256,256]{3,2,1,0:T(8,128)(2,1)} %constant.21.clone.dft_ref) | copy-start | bytes 3145732
  89.1 25.1 %copy-start.3 = (f32[2,512,128]{2,1,0:T(8,128)S(1)}, f32[2,512,128]{2,1,0:T(8,128)}, u32[]{:S(2)}) copy-start(f32[2,512,128]{2,1,0:T(8,128)} %constant.23.clone.turn_ref) | copy-start | bytes 1572868
  89.1 25.1 %copy-start.4 = (f32[2,256,128]{2,1,0:T(8,128)S(1)}, f32[2,256,128]{2,1,0:T(8,128)}, u32[]{:S(2)}) copy-start(f32[2,256,128]{2,1,0:T(8,128)} %constant.22.clone.middle_ref) | copy-start | bytes 786436
  145.5 87.1 %copy-start.5 = (bf16[256,128]{1,0:T(8,128)(2,1)S(1)}, bf16[256,128]{1,0:T(8,128)(2,1)}, u32[]{:S(2)}) copy-start(bf16[256,128]{1,0:T(8,128)(2,1)} %constant.24.clone.table_ref) | copy-start | bytes 196612
  232.6 15.7 %copy-start.6 = (s32[96,96]{1,0:T(8,128)S(1)}, s32[96,96]{1,0:T(8,128)}, u32[]{:S(2)}) copy-start(s32[96,96]{1,0:T(8,128)} %starts_ref.1) | copy-start | bytes 110596
  232.6 15.7 %copy-start.7 = (s32[96,96]{1,0:T(8,128)S(1)}, s32[96,96]{1,0:T(8,128)}, u32[]{:S(2)}) copy-start(s32[96,96]{1,0:T(8,128)} %lengths_ref.1) | copy-start | bytes 110596
  233.3 29.1 %copy-start.2 = (bf16[2,12,2,8192]{3,2,1,0:T(2,128)(2,1)S(1)}, bf16[2,12,2,8192]{3,2,1,0:T(2,128)(2,1)}, u32[]{:S(2)}) copy-start(bf16[2,12,2,8192]{3,2,1,0:T(2,128)(2,1)} %param.10) | copy-start | bytes 2359300

commit v7 on v6

--- a/solution.py
+++ b/solution.py
@@ -223,15 +223,24 @@
             work[part, half:OUTER] = even[part] - odd[part]
             work[part, OUTER : OUTER + REACH] = work[part, OUTER - REACH : OUTER]
             work[part, OUTER + REACH :] = work[part, :REACH]
-        work[0], work[1] = turned(work[0], work[1], own_ref[0], own_ref[1], 1)
         for group in range(8):
             low, high = 64 * group, 64 * group + 64
             before = low - REACH if group else OUTER
             after = high if group < 7 else OUTER + REACH
-            for part in range(2):
-                out_ref[group, part, row, :64] = work[part, low:high]
-                out_ref[group, part, row, 64 : 64 + REACH] = work[part, before : before + REACH]
-                out_ref[group, part, row, 64 + REACH :] = work[part, after : after + REACH]
+            for start, stop, to in (
+                (low, high, 0),
+                (before, before + REACH, 64),
+                (after, after + REACH, 64 + REACH),
+            ):
+                fields = turned(
+                    work[0, start:stop],
+                    work[1, start:stop],
+                    own_ref[0, start:stop],
+                    own_ref[1, start:stop],
+                    1,
+                )
+                for part in range(2):
+                    out_ref[group, part, row, to : to + stop - start] = fields[part]
 
 
 def disperse(values, own):

time: 265 us -> 265 us (level)
  no operation moved by 1% of the time
where the time goes in v7:
time: 265 us
  blocking collectives  252 us (95%)
  Pallas kernels  11.1 us (4%)
    all_to_all x6, blocking collectives, exchange(): return lax.all_to_all(values, axis, 0, 0, tiled=True)  252 us
    pallas_call x1, Pallas kernels, disperse(): pl.pallas_call(disperse_kernel, in_specs=[vmem] * 5, out_specs=vmem, out_...  5.69 us

profile of v7, /device:TPU:2, one launch (start us, length us, event | category | flops | bytes accessed | tf_op | source)
XLA Modules:
  0.0 264.7 jit_solution(11409162395493676661)
XLA Ops:
  0.0 1.4 dynamic-slice_bitcast_fusion.tables_ref.own_ref
  1.4 0.3 copy-done
  1.7 0.1 head.1
  1.8 87.0 %all_to_all.30.in_ref = f32[8,2,3,64,128]{4,3,2,1,0:T(8,128)S(1)} all-to-all(f32[8,2,3,64,128]{4,3,2,1,0:T(8,128)S(1)} %head.1), channel_id=1, replica_groups=mesh['chan'=8,'j'=8,'i'=8] {'j'}, dimensions={0} | all-to-all | bytes 3145728 | tf_op jit(solution)/shard_map/all_to_all | solution.py:525
  88.8 0.3 fold.1
  89.1 0.0 copy-start.1
  89.1 0.0 copy-start.3
  89.1 0.0 copy-start.4
  89.1 25.1 %all_to_all.31.in_ref = f32[8,2,3,64,128]{4,3,2,1,0:T(8,128)S(1)} all-to-all(f32[8,2,3,64,128]{4,3,2,1,0:T(8,128)S(1)} %fold.1), channel_id=1, replica_groups=mesh['chan'=8,'j'=8,'i'=8] {'i'}, dimensions={0} | all-to-all | bytes 3145728 | tf_op jit(solution)/shard_map/all_to_all | solution.py:525
  114.2 0.0 copy-done.1
  114.2 0.0 copy-done.3
  114.2 0.0 copy-done.4
  114.2 5.7 %disperse.1 = f32[8,2,3,72,128]{4,3,2,1,0:T(8,128)S(1)} custom-call(f32[8,2,3,64,128]{4,3,2,1,0:T(8,128)S(1)} %all_to_all.31.in_ref, bf16[4,2,256,256]{3,2,1,0:T(8,128)(2,1)S(1)} %copy-done.1, f32[2,256,128]{2,1,0:T(8,128)S(1)} %copy-done.4, f32[2,512,128]{2,1,0:T(8,128)S(1)} %copy-done.3, f32[4,520,128]{2,1,0:T(8,128)S(1)} %dynamic-slice_bitcast_fusion.tables_ref.own_ref), custom_call_target="tpu_custom_call" | custom-call | tf_op jit(solution)/shard_map/disperse/pallas_call | solution.py:250
  119.9 25.4 %all_to_all.32.in_ref = f32[8,2,3,72,128]{4,3,2,1,0:T(8,128)S(1)} all-to-all(f32[8,2,3,72,128]{4,3,2,1,0:T(8,128)S(1)} %disperse.1), channel_id=1, replica_groups=mesh['chan'=8,'j'=8,'i'=8] {'i'}, dimensions={0} | all-to-all | bytes 3538944 | tf_op jit(solution)/shard_map/all_to_all | solution.py:525
  145.3 0.3 unfold.1
  145.5 0.0 copy-start.5
  145.5 87.1 %all_to_all.33.held = f32[8,400,128]{2,1,0:T(8,128)S(1)} all-to-all(f32[8,400,128]{2,1,0:T(8,128)S(1)} %unfold.1), channel_id=1, replica_groups=mesh['chan'=8,'j'=8,'i'=8] {'j'}, dimensions={0} | all-to-all | bytes 3276800 | tf_op jit(solution)/shard_map/all_to_all | solution.py:525
  232.6 0.7 slide.1
  233.3 0.0 copy-start.2
  233.3 15.0 %all_to_all.34.in_ref = f32[8,112,128]{2,1,0:T(8,128)S(1)} all-to-all(f32[8,112,128]{2,1,0:T(8,128)S(1)} %slide.1), channel_id=1, replica_groups=mesh['chan'=8,'j'=8,'i'=8] {'chan'}, dimensions={0} | all-to-all | bytes 917504 | tf_op jit(solution)/shard_map/all_to_all | solution.py:525
  248.3 1.8 cross.1
  250.1 12.3 %all_to_all.35.cross_ref = f32[8,96,128]{2,1,0:T(8,128)S(1)} all-to-all(f32[8,96,128]{2,1,0:T(8,128)S(1)} %bitcast.18), channel_id=1, replica_groups=mesh['chan'=8,'j'=8,'i'=8] {'chan'}, dimensions={0} | all-to-all | bytes 786432 | tf_op jit(solution)/shard_map/all_to_all | solution.py:525
  262.4 0.0 copy-done.2
  262.4 2.3 tail.1
  (6 shorter events, 0.0 us)
Async XLA Ops:
  0.0 1.7 copy-start
  89.1 25.1 %copy-start.1 = (bf16[4,2,256,256]{3,2,1,0:T(8,128)(2,1)S(1)}, bf16[4,2,256,256]{3,2,1,0:T(8,128)(2,1)}, u32[]{:S(2)}) copy-start(bf16[4,2,256,256]{3,2,1,0:T(8,128)(2,1)} %constant.21.clone.dft_ref) | copy-start | bytes 3145732
  89.1 25.1 %copy-start.3 = (f32[2,512,128]{2,1,0:T(8,128)S(1)}, f32[2,512,128]{2,1,0:T(8,128)}, u32[]{:S(2)}) copy-start(f32[2,512,128]{2,1,0:T(8,128)} %constant.23.clone.turn_ref) | copy-start | bytes 1572868
  89.1 25.1 %copy-start.4 = (f32[2,256,128]{2,1,0:T(8,128)S(1)}, f32[2,256,128]{2,1,0:T(8,128)}, u32[]{:S(2)}) copy-start(f32[2,256,128]{2,1,0:T(8,128)} %constant.22.clone.middle_ref) | copy-start | bytes 786436
  145.5 87.1 %copy-start.5 = (bf16[256,128]{1,0:T(8,128)(2,1)S(1)}, bf16[256,128]{1,0:T(8,128)(2,1)}, u32[]{:S(2)}) copy-start(bf16[256,128]{1,0:T(8,128)(2,1)} %constant.24.clone.table_ref) | copy-start | bytes 196612
  232.6 15.7 %copy-start.6 = (s32[96,96]{1,0:T(8,128)S(1)}, s32[96,96]{1,0:T(8,128)}, u32[]{:S(2)}) copy-start(s32[96,96]{1,0:T(8,128)} %starts_ref.1) | copy-start | bytes 110596
  232.6 15.7 %copy-start.7 = (s32[96,96]{1,0:T(8,128)S(1)}, s32[96,96]{1,0:T(8,128)}, u32[]{:S(2)}) copy-start(s32[96,96]{1,0:T(8,128)} %lengths_ref.1) | copy-start | bytes 110596
  233.3 29.1 %copy-start.2 = (bf16[2,12,2,8192]{3,2,1,0:T(2,128)(2,1)S(1)}, bf16[2,12,2,8192]{3,2,1,0:T(2,128)(2,1)}, u32[]{:S(2)}) copy-start(bf16[2,12,2,8192]{3,2,1,0:T(2,128)(2,1)} %param.10) | copy-start | bytes 2359300
